TPU v7x, 128 devices: a whole 4x4x4 slice. The times are simulated.
128 devices in a mesh: node: 16 (over z, y), local: 8 (over x, core).
Axes of the slice: x: 4, y: 4, z: 4, core: 2. Of those that a mesh axis runs over, the one named last changes fastest.
Arguments:
- tokens: bfloat16 [16384, 3584], P(('node', 'local')), may hold values from -6 to 6
- cotangent: bfloat16 [16384, 3584], P(('node', 'local')), may hold values from -0.75 to 0.75
- expert_ids: int32 [16384, 8], P(('node', 'local')), may hold values from 0 to 127, as said below
- gate_fixed: int32 [16384, 8], P(('node', 'local')), may hold values from 1 to 65535
- w_up: bfloat16 [128, 3584, 1024], P(('node', 'local')), may hold values from -0.09375 to 0.09375
- w_down: bfloat16 [128, 1024, 3584], P(('node', 'local')), may hold values from -0.1875 to 0.1875
Outputs:
- grad_input: bfloat16 [16384, 3584], P(('node', 'local'))
- grad_gate: bfloat16 [16384, 8], P(('node', 'local'))
Inputs may be any that keep to these rules, and one draw needn't show every extreme that they name: `expert_ids`: expert e belongs to node group e // 8 (the group of devices with one index of node). Each row names 8 different experts, exactly two in each of 4 different node groups. In the 128 rows of one device every node group is named by exactly 32 rows, and no expert is named by more than 10 rows.
All inputs are finite; a program needn't handle non-finite values.
Results may differ from a plain program's by a relative error of at most 0.013.
Values may be sent and summed in bfloat16 or wider, within the bound.
No kernel may reach another device: no remote copies, remote signals or barrier semaphores. Data moves between devices by JAX's collectives and lax.ppermute only.
A program may use at most 192 MiB of HBM per device.

v0:
```python
import jax
import jax.numpy as jnp
from jax import lax
from jax.sharding import PartitionSpec as P

NODES_MAX = 4


def per_device(tokens, cotangent, expert_ids, gate_fixed, w_up, w_down):
    node_count = lax.axis_size("node")
    local_count = lax.axis_size("local")
    experts = node_count * local_count
    tok_rows = tokens.shape[0]
    width = tokens.shape[1]
    top = expert_ids.shape[1]
    share = tok_rows * NODES_MAX // node_count
    spots = 2 * share
    period = 4 * local_count + 1
    offsets = [0, local_count // 2, local_count + 1, 2 * local_count + 1, 3 * local_count + 1]
    capacity = max(2, sum([(spots - start_pos + period - 1) // period for start_pos in offsets]))
    padded_x = jnp.concatenate([tokens, jnp.zeros((1, width), tokens.dtype)], axis=0)
    padded_dy = jnp.concatenate([cotangent, jnp.zeros((1, width), cotangent.dtype)], axis=0)
    up_w = w_up[0]
    down_w = w_down[0]
    hits = jnp.sum(
        (expert_ids[:, :, None] == jnp.arange(experts, dtype=jnp.int32)[None, None, :]).astype(
            jnp.int32
        ),
        axis=1,
    )
    before = jnp.cumsum(hits, axis=0) - hits
    position = jnp.take_along_axis(before, expert_ids, axis=1)
    flat = expert_ids * capacity + position
    owner = (
        jnp.full((experts * capacity,), tok_rows, jnp.int32)
        .at[flat.reshape(-1)]
        .set(jnp.repeat(jnp.arange(tok_rows, dtype=jnp.int32), top))
    )
    send_x = padded_x[owner].reshape(experts, capacity, width)
    send_dy = padded_dy[owner].reshape(experts, capacity, width)
    flat, send_x, send_dy = (flat, send_x, send_dy)
    rows_x = lax.all_to_all(send_x, ("node", "local"), split_axis=0, concat_axis=0, tiled=True)
    rows_dy = lax.all_to_all(send_dy, ("node", "local"), split_axis=0, concat_axis=0, tiled=True)
    leading = rows_x.shape[:-1]
    rows_x = rows_x.reshape(-1, width)
    rows_dy = rows_dy.reshape(-1, width)
    pre = jnp.dot(rows_x, up_w, preferred_element_type=jnp.float32)
    act = jax.nn.silu(pre).astype(jnp.bfloat16)
    back = jnp.einsum("rd,hd->rh", rows_dy, down_w, preferred_element_type=jnp.float32)
    gate_grad = jnp.sum(act.astype(jnp.float32) * back, axis=-1).astype(jnp.bfloat16)
    sig = jax.nn.sigmoid(pre)
    inner = (back * sig * (1.0 + pre * (1.0 - sig))).astype(jnp.bfloat16)
    piece = jnp.einsum("rh,dh->rd", inner, up_w, preferred_element_type=jnp.float32).astype(
        jnp.bfloat16
    )
    returned = (
        lax.all_to_all(
            piece.reshape(leading + (width,)),
            ("node", "local"),
            split_axis=0,
            concat_axis=0,
            tiled=True,
        ),
        lax.all_to_all(
            gate_grad.reshape(leading), ("node", "local"), split_axis=0, concat_axis=0, tiled=True
        ),
    )
    grads_flat = returned[0].reshape(experts * capacity, width)
    gates_flat = returned[1].reshape(experts * capacity)
    pieces = grads_flat[flat]
    scale = gate_fixed.astype(jnp.float32) / 65536.0
    grad_input = jnp.sum(scale[:, :, None] * pieces.astype(jnp.float32), axis=1).astype(
        jnp.bfloat16
    )
    grad_gate = gates_flat[flat]
    return (grad_input, grad_gate)


def solution(mesh):
    placed = (
        P(("node", "local"), None),
        P(("node", "local"), None),
        P(("node", "local"), None),
        P(("node", "local"), None),
        P(("node", "local"), None, None),
        P(("node", "local"), None, None),
    )
    return jax.shard_map(
        per_device,
        mesh=mesh,
        in_specs=placed,
        out_specs=(P(("node", "local"), None), P(("node", "local"), None)),
        check_vma=False,
    )
```

profile of v0, /device:TPU:84, one launch (start us, length us, event | category | flops | bytes accessed | tf_op | source)
XLA Modules:
  0.0 797.2 jit_solution(5736623122789138423)
XLA Ops:
  2.7 6.8 gather_fusion.4
  10.6 4.3 scatter_custom_fusion
  15.1 7.9 gather_fusion.1
  23.0 14.2 %reshape.91 = bf16[128,10,3584]{2,1,0:T(8,128)(2,1)} reshape(bf16[1280,3584]{1,0:T(8,128)(2,1)} %gather_fusion.1) | data formatting | bytes 18350080 | tf_op jit(solution)/shard_map/reshape | solution.py:39
  37.2 10.3 %all-to-all-start.1 = ((bf16[128,10,3584]{2,1,0:T(8,128)(2,1)}), bf16[128,10,3584]{2,1,0:T(8,128)(2,1)}, u32[]{:S(2)}, u32[]{:S(2)}) async-start(bf16[128,10,3584]{2,1,0:T(8,128)(2,1)} %reshape.91), calls=%async_computation.1 | async-start | bytes 29360128 | tf_op jit(solution)/shard_map/all_to_all | solution.py:42
  47.7 7.8 gather_fusion
  55.5 14.2 %reshape.89 = bf16[128,10,3584]{2,1,0:T(8,128)(2,1)} reshape(bf16[1280,3584]{1,0:T(8,128)(2,1)} %gather_fusion) | data formatting | bytes 18350080 | tf_op jit(solution)/shard_map/reshape | solution.py:40
  69.7 177.8 %all-to-all-done.1 = bf16[128,10,3584]{2,1,0:T(8,128)(2,1)} async-done(((bf16[128,10,3584]{2,1,0:T(8,128)(2,1)}), bf16[128,10,3584]{2,1,0:T(8,128)(2,1)}, u32[]{:S(2)}, u32[]{:S(2)}) %all-to-all-start.1) | async-done | bytes 9175072 | tf_op jit(solution)/shard_map/all_to_all | solution.py:42
  247.5 10.8 %all-to-all-start = ((bf16[128,10,3584]{2,1,0:T(8,128)(2,1)}), bf16[128,10,3584]{2,1,0:T(8,128)(2,1)}, u32[]{:S(2)}, u32[]{:S(2)}) async-start(bf16[128,10,3584]{2,1,0:T(8,128)(2,1)} %reshape.89), calls=%async_computation | async-start | bytes 29360128 | tf_op jit(solution)/shard_map/all_to_all | solution.py:43
  258.3 14.7 %reshape.92 = bf16[1280,3584]{1,0:T(8,128)(2,1)} reshape(bf16[128,10,3584]{2,1,0:T(8,128)(2,1)} %all-to-all-done.1) | data formatting | bytes 18350080 | tf_op jit(solution)/shard_map/reshape | solution.py:45
  273.0 15.7 %fusion.2 = f32[1280,1024]{0,1:T(8,128)} fusion(bf16[1280,3584]{1,0:T(8,128)(2,1)} %reshape.92, bf16[1,3584,1024]{2,1,0:T(8,128)(2,1)} %param.10), kind=kOutput, calls=%fused_computation.10 | convolution fusion | flops 9395240960 | bytes 21757952 | tf_op jit(solution)/shard_map/dot_general | solution.py:47
  288.7 173.4 %all-to-all-done = bf16[128,10,3584]{2,1,0:T(8,128)(2,1)} async-done(((bf16[128,10,3584]{2,1,0:T(8,128)(2,1)}), bf16[128,10,3584]{2,1,0:T(8,128)(2,1)}, u32[]{:S(2)}, u32[]{:S(2)}) %all-to-all-start) | async-done | bytes 9175072 | tf_op jit(solution)/shard_map/all_to_all | solution.py:43
  462.1 14.7 %reshape.90 = bf16[1280,3584]{1,0:T(8,128)(2,1)} reshape(bf16[128,10,3584]{2,1,0:T(8,128)(2,1)} %all-to-all-done) | data formatting | bytes 18350080 | tf_op jit(solution)/shard_map/reshape | solution.py:46
  476.8 17.1 %multiply_reduce_fusion = (bf16[1280]{0:T(1024)(128)(2,1)S(1)}, f32[1280,1024]{0,1:T(8,128)}) fusion(f32[1280,1024]{0,1:T(8,128)} %fusion.2, bf16[1280,3584]{1,0:T(8,128)(2,1)} %reshape.90, bf16[1,1024,3584]{2,1,0:T(8,128)(2,1)} %param.11), kind=kOutput, calls=%fused_computation.14 | convolution fusion | flops 9405725696 | bytes 27003392 | tf_op jit(solution)/shard_map/rd,hd->rh/dot_general | solution.py:49
  493.9 0.8 convert_element_type.49
  494.7 9.8 %all-to-all-start.3 = ((bf16[128,1,10]{2,1,0:T(2,128)(2,1)}), bf16[128,1,10]{2,1,0:T(2,128)(2,1)S(1)}, u32[]{:S(2)}, u32[]{:S(2)}) async-start(bf16[128,1,10]{2,1,0:T(2,128)(2,1)} %convert_element_type.49), calls=%async_computation.3 | async-start | bytes 131072 | tf_op jit(solution)/shard_map/all_to_all | solution.py:64
  504.5 20.6 %convolution_convert_fusion = bf16[1280,3584]{1,0:T(8,128)(2,1)} fusion(bf16[1,3584,1024]{2,1,0:T(8,128)(2,1)} %param.10, f32[1280,1024]{0,1:T(8,128)} %fusion.2, f32[1280,1024]{0,1:T(8,128)} %get-tuple-element.13), kind=kOutput, calls=%fused_computation.6 | convolution fusion | flops 9411624960 | bytes 27000832 | tf_op jit(solution)/shard_map/rh,dh->rd/dot_general | solution.py:53
  525.1 14.2 %reshape.93 = bf16[128,10,3584]{2,1,0:T(8,128)(2,1)} reshape(bf16[1280,3584]{1,0:T(8,128)(2,1)} %convolution_convert_fusion) | data formatting | bytes 18350080 | tf_op jit(solution)/shard_map/reshape | solution.py:58
  539.4 10.2 %all-to-all-start.2 = ((bf16[128,10,3584]{2,1,0:T(8,128)(2,1)}), bf16[128,10,3584]{2,1,0:T(8,128)(2,1)}, u32[]{:S(2)}, u32[]{:S(2)}) async-start(bf16[128,10,3584]{2,1,0:T(8,128)(2,1)} %reshape.93), calls=%async_computation.2 | async-start | bytes 29360128 | tf_op jit(solution)/shard_map/all_to_all | solution.py:57
  550.2 6.8 gather_fusion.3
  557.8 195.5 %all-to-all-done.2 = bf16[128,10,3584]{2,1,0:T(8,128)(2,1)} async-done(((bf16[128,10,3584]{2,1,0:T(8,128)(2,1)}), bf16[128,10,3584]{2,1,0:T(8,128)(2,1)}, u32[]{:S(2)}, u32[]{:S(2)}) %all-to-all-start.2) | async-done | bytes 9175072 | tf_op jit(solution)/shard_map/all_to_all | solution.py:57
  753.3 14.6 %reshape.94 = bf16[1280,3584]{1,0:T(8,128)(2,1)} reshape(bf16[128,10,3584]{2,1,0:T(8,128)(2,1)} %all-to-all-done.2) | data formatting | bytes 18350080 | tf_op jit(solution)/shard_map/reshape | solution.py:68
  767.9 18.6 %gather_fusion.2 = bf16[1024,3584]{1,0:T(8,128)(2,1)} fusion(bf16[1280,3584]{1,0:T(8,128)(2,1)} %reshape.94, s32[1024]{0:T(1024)S(1)} %broadcast_clamp_fusion), kind=kCustom, calls=%fused_computation.2 | custom fusion | bytes 14684160 | tf_op jit(solution)/shard_map/gather | solution.py:70
  786.5 10.7 %fusion = bf16[128,3584]{1,0:T(8,128)(2,1)} fusion(bf16[1024,3584]{1,0:T(8,128)(2,1)} %gather_fusion.2, f32[128,8]{1,0:T(8,128)S(1)} %copy.42), kind=kLoop, calls=%fused_computation.8 | loop fusion | flops 10551296 | bytes 8261632 | tf_op jit(solution)/shard_map/reduce_sum | solution.py:72
  (39 shorter events, 4.7 us)
Async XLA Ops:
  2.7 7.0 copy-start.2
  2.7 12.3 %copy-start = (bf16[128,3584]{1,0:T(8,128)(2,1)S(1)}, bf16[128,3584]{1,0:T(8,128)(2,1)}, u32[]{:S(2)}) copy-start(bf16[128,3584]{1,0:T(8,128)(2,1)} %param.6) | copy-start | bytes 2752516
  37.2 10.3 %copy-start.1 = (bf16[128,3584]{1,0:T(8,128)(2,1)S(1)}, bf16[128,3584]{1,0:T(8,128)(2,1)}, u32[]{:S(2)}) copy-start(bf16[128,3584]{1,0:T(8,128)(2,1)} %param.7) | copy-start | bytes 2752516
  37.2 210.2 %all-to-all-start.1 = ((bf16[128,10,3584]{2,1,0:T(8,128)(2,1)}), bf16[128,10,3584]{2,1,0:T(8,128)(2,1)}, u32[]{:S(2)}, u32[]{:S(2)}) async-start(bf16[128,10,3584]{2,1,0:T(8,128)(2,1)} %reshape.91), calls=%async_computation.1 | async-start | bytes 29360128 | tf_op jit(solution)/shard_map/all_to_all | solution.py:42
  247.5 214.6 %all-to-all-start = ((bf16[128,10,3584]{2,1,0:T(8,128)(2,1)}), bf16[128,10,3584]{2,1,0:T(8,128)(2,1)}, u32[]{:S(2)}, u32[]{:S(2)}) async-start(bf16[128,10,3584]{2,1,0:T(8,128)(2,1)} %reshape.89), calls=%async_computation | async-start | bytes 29360128 | tf_op jit(solution)/shard_map/all_to_all | solution.py:43
  494.7 44.7 %all-to-all-start.3 = ((bf16[128,1,10]{2,1,0:T(2,128)(2,1)}), bf16[128,1,10]{2,1,0:T(2,128)(2,1)S(1)}, u32[]{:S(2)}, u32[]{:S(2)}) async-start(bf16[128,1,10]{2,1,0:T(2,128)(2,1)} %convert_element_type.49), calls=%async_computation.3 | async-start | bytes 131072 | tf_op jit(solution)/shard_map/all_to_all | solution.py:64
  539.4 10.2 %copy-start.3 = (s32[128,8]{0,1:T(8,128)S(1)}, s32[128,8]{0,1:T(8,128)}, u32[]{:S(2)}) copy-start(s32[128,8]{0,1:T(8,128)} %get-tuple-element.10) | copy-start | bytes 12292
  539.4 10.4 %copy-start.4 = (s32[128,8]{0,1:T(8,128)S(1)}, s32[128,8]{0,1:T(8,128)}, u32[]{:S(2)}) copy-start(s32[128,8]{0,1:T(8,128)} %param.9) | copy-start | bytes 12292
  539.4 213.9 %all-to-all-start.2 = ((bf16[128,10,3584]{2,1,0:T(8,128)(2,1)}), bf16[128,10,3584]{2,1,0:T(8,128)(2,1)}, u32[]{:S(2)}, u32[]{:S(2)}) async-start(bf16[128,10,3584]{2,1,0:T(8,128)(2,1)} %reshape.93), calls=%async_computation.2 | async-start | bytes 29360128 | tf_op jit(solution)/shard_map/all_to_all | solution.py:57
where the time goes:
time: 800 us; the launch traced here: 797 us
  waiting for transfers between devices  547 us (68%)
  local copies, waits for them, and re-layouts  142 us (18%)
  matrix products  53.5 us (7%)
  starting transfers between devices  41.1 us (5%)
  other arithmetic  12.7 us (2%)
    all_to_all x1, waiting for transfers between devices, per_device(): lax.all_to_all(piece.reshape(leading + (width,)), ('node', 'local'), spli...  196 us
    all_to_all x1, waiting for transfers between devices, per_device(): lax.all_to_all(send_x, ('node', 'local'), split_axis=0, concat_axis=0, ti...  178 us
    all_to_all x1, waiting for transfers between devices, per_device(): lax.all_to_all(send_dy, ('node', 'local'), split_axis=0, concat_axis=0, t...  173 us
    dot_general x1, matrix products, per_device(): jnp.einsum('rh,dh->rd', inner, up_w, preferred_element_type=jnp.float32)  20.6 us
    gather x1, local copies, waits for them, and re-layouts, per_device(): pieces = grads_flat[flat]  18.6 us
    dot_general x1, matrix products, per_device(): jnp.einsum('rd,hd->rh', rows_dy, down_w, preferred_element_type=jnp.float32)  17.1 us
  transfers between devices with their start and end apart: 4, of which 3 were waited for; matrix products, arithmetic and copies ran while one was open for 12% of the time, Pallas kernels for 0%

commit v1 on v0

v1 whole, which is shorter than its diff:
```python
import jax
import jax.numpy as jnp
from jax import lax
from jax.experimental import pallas as pl
from jax.experimental.pallas import tpu as pltpu
from jax.sharding import PartitionSpec as P

CAP = 10
MAIN = 8
QUARTERS = 4
GROUP = 32
EXTRA = 128
VMEM = 56 * 1024 * 1024
BF16 = jnp.bfloat16
F32 = jnp.float32


def iota(shape, dim):
    return lax.broadcasted_iota(jnp.int32, shape, dim)


def dot(a, b):
    return jnp.dot(a, b, preferred_element_type=F32)


def dot_nt(a, b):
    return lax.dot_general(a, b, (((1,), (1,)), ((), ())), preferred_element_type=F32)


def dot_tn(a, b):
    return lax.dot_general(a, b, (((0,), (0,)), ((), ())), preferred_element_type=F32)


def slots_of(ids, first):
    tok = ids.shape[1]
    expert = first + iota((GROUP, tok), 0)
    hit = jnp.zeros((GROUP, tok), F32)
    for slot in range(ids.shape[0]):
        hit = hit + (expert == ids[slot : slot + 1, :]).astype(F32)
    earlier = (iota((tok, tok), 0) < iota((tok, tok), 1)).astype(BF16)
    before = dot(hit.astype(BF16), earlier)
    place = jnp.where(hit > 0.5, before, -1.0)
    rows = GROUP * MAIN
    spread = (iota((rows, GROUP), 0) // MAIN == iota((rows, GROUP), 1)).astype(BF16)
    return dot(spread, place.astype(BF16)), spread, expert


def picks(ids, first):
    place, spread, expert = slots_of(ids, first)
    row = iota(place.shape, 0)
    main = place == (row % MAIN).astype(F32)
    tail = place == (MAIN + row % 2).astype(F32)
    quarter = (row % MAIN) // 2
    return main, tail, quarter, spread, expert


def send_kernel(ids_ref, x_ref, out_ref):
    width = x_ref.shape[1]
    fold = width // QUARTERS
    main, tail, quarter, _, _ = picks(ids_ref[...], pl.program_id(0) * GROUP)
    out_ref[:, :width] = dot(main.astype(BF16), x_ref[...]).astype(BF16)
    total = None
    for q in range(QUARTERS):
        pick = jnp.logical_and(tail, quarter == q).astype(BF16)
        part = dot(pick, x_ref[:, q * fold : (q + 1) * fold])
        total = part if total is None else total + part
    out_ref[:, width:] = total.astype(BF16)


def send(ids_t, x):
    tok, width = x.shape
    experts = lax.axis_size("node") * lax.axis_size("local")
    wide = width + width // QUARTERS
    rows = GROUP * MAIN
    return pl.pallas_call(
        send_kernel,
        grid=(experts // GROUP,),
        in_specs=[
            pl.BlockSpec(ids_t.shape, lambda i: (0, 0)),
            pl.BlockSpec((tok, width), lambda i: (0, 0)),
        ],
        out_specs=pl.BlockSpec((rows, wide), lambda i: (i, 0)),
        out_shape=jax.ShapeDtypeStruct((experts * MAIN, wide), BF16),
        compiler_params=pltpu.CompilerParams(vmem_limit_bytes=VMEM),
        cost_estimate=pl.CostEstimate(
            flops=4 * experts * MAIN * 256 * width, bytes_accessed=2 * experts * MAIN * wide, transcendentals=0
        ),
        name="pick_rows",
    )(ids_t, x)


def unfold(rows_ref, tail_ref, width):
    fold = width // QUARTERS
    size = GROUP * MAIN
    tails = 2 * GROUP
    to = iota((size, size), 0)
    source = ((to % tails) // 2) * MAIN + (to // tails) * 2 + to % 2
    order = (source == iota((size, size), 1)).astype(BF16)
    for b in range(rows_ref.shape[0] // size):
        stack = dot(order, rows_ref[b * size : (b + 1) * size, width : width + fold]).astype(BF16)
        for q in range(QUARTERS):
            tail_ref[b * tails : (b + 1) * tails, q * fold : (q + 1) * fold] = stack[q * tails : (q + 1) * tails, :]


def pre_kernel(rows_ref, w_ref, out_ref, tail_ref):
    width = w_ref.shape[0]
    main = rows_ref.shape[0]

    @pl.when(pl.program_id(0) == 0)
    def _():
        unfold(rows_ref, tail_ref, width)

    out_ref[:main, :] = dot(rows_ref[:, :width], w_ref[...])
    out_ref[main:, :] = dot(tail_ref[...], w_ref[...])


def pre_of(rows, w_up, tile=256):
    main, wide = rows.shape
    width, hid = w_up.shape
    tails = main // QUARTERS
    return pl.pallas_call(
        pre_kernel,
        grid=(hid // tile,),
        in_specs=[
            pl.BlockSpec((main, wide), lambda i: (0, 0), pipeline_mode=pl.Buffered(1)),
            pl.BlockSpec((width, tile), lambda i: (0, i)),
        ],
        out_specs=pl.BlockSpec((main + tails, tile), lambda i: (0, i)),
        out_shape=jax.ShapeDtypeStruct((main + tails, hid), F32),
        scratch_shapes=[pltpu.VMEM((tails, width), BF16)],
        compiler_params=pltpu.CompilerParams(vmem_limit_bytes=VMEM),
        cost_estimate=pl.CostEstimate(
            flops=2 * (main + tails) * width * hid, bytes_accessed=22_000_000, transcendentals=0
        ),
        name="pre",
    )(rows, w_up)


def back_kernel(
    rows_ref, pre_ref, down_ref, up_ref, out_ref, tail_ref, inner_ref, gate_ref, piece_ref, stack_ref, fold_ref, extra_ref, sems
):
    step = pl.program_id(0)
    width = down_ref.shape[1]
    tile = down_ref.shape[0]
    hid = inner_ref.shape[1]
    main = rows_ref.shape[0]
    fold = width // QUARTERS
    tails = 2 * GROUP
    size = GROUP * MAIN
    groups = main // size
    first = hid // tile

    @pl.when(step == 0)
    def _():
        unfold(rows_ref, tail_ref, width)

    def hidden(rows, where):
        pre = pre_ref[where, :]
        back = dot_nt(rows, down_ref[...])
        sig = 1.0 / (1.0 + jnp.exp(-pre))
        act = (pre * sig).astype(BF16).astype(F32)
        inner = (back * sig * (1.0 + pre * (1.0 - sig))).astype(BF16)
        return inner, jnp.sum(act * back, axis=-1, keepdims=True)

    for j in range(first):

        @pl.when(step == j)
        def _():
            for where, rows in ((slice(0, main), rows_ref[:, :width]), (slice(main, None), tail_ref[...])):
                inner, gate = hidden(rows, where)
                inner_ref[where, j * tile : (j + 1) * tile] = inner
                if j == 0:
                    gate_ref[where, :] = gate
                else:
                    gate_ref[where, :] = gate_ref[where, :] + gate

    def copy_of(q):
        return pltpu.make_async_copy(
            piece_ref.at[q % 2], out_ref.at[:, pl.ds(q * fold, fold)], sems.at[q % 2]
        )

    fold_copy = pltpu.make_async_copy(fold_ref, out_ref.at[:, pl.ds(width, fold)], sems.at[2])
    extra_copy = pltpu.make_async_copy(extra_ref, out_ref.at[:, pl.ds(width + fold, EXTRA)], sems.at[3])

    for q in range(QUARTERS):

        @pl.when(step == first + q)
        def _():
            if q >= 2:
                copy_of(q - 2).wait()
            piece_ref[q % 2] = dot_nt(inner_ref[:main, :], up_ref[...]).astype(BF16)
            copy_of(q).start()
            if q == 0:
                pick = (iota((size, tails), 0) // MAIN == iota((size, tails), 1) // 2).astype(BF16)
                parity = iota((size, EXTRA), 0) % 2
                low = iota((size, EXTRA), 1) < EXTRA // 2
                for b in range(groups):
                    mains = gate_ref[b * size : (b + 1) * size, :].astype(BF16).astype(F32)
                    last = gate_ref[main + b * tails : main + (b + 1) * tails, :].astype(BF16).astype(F32)
                    odd = (iota((tails, EXTRA), 0) % 2 == 1)
                    last = jnp.broadcast_to(last, (tails, EXTRA))
                    even_rows = dot(pick, jnp.where(odd, 0.0, last).astype(BF16))
                    odd_rows = dot(pick, jnp.where(odd, last, 0.0).astype(BF16))
                    tail_rows = jnp.where(parity == 1, odd_rows, even_rows)
                    extra_ref[b * size : (b + 1) * size, :] = jnp.where(
                        low, jnp.broadcast_to(mains, (size, EXTRA)), tail_rows
                    ).astype(BF16)
                extra_copy.start()
            piece = dot_nt(inner_ref[main:, :], up_ref[...]).astype(BF16)
            for b in range(groups):
                stack_ref[b * size + q * tails : b * size + (q + 1) * tails, :] = piece[b * tails : (b + 1) * tails, :]
            if q == QUARTERS - 1:
                to = iota((size, size), 0)
                source = ((to % MAIN) // 2) * tails + (to // MAIN) * 2 + to % 2
                order = (source == iota((size, size), 1)).astype(BF16)
                for b in range(groups):
                    fold_ref[b * size : (b + 1) * size, :] = dot(
                        order, stack_ref[b * size : (b + 1) * size, :]
                    ).astype(BF16)
                fold_copy.start()
                copy_of(q - 1).wait()
                copy_of(q).wait()
                extra_copy.wait()
                fold_copy.wait()


def pieces_of(rows, pre, w_down, w_up, tile=256):
    main, wide = rows.shape
    hid, width = w_down.shape
    tails = main // QUARTERS
    fold = width // QUARTERS
    first = hid // tile
    return pl.pallas_call(
        back_kernel,
        grid=(first + QUARTERS,),
        in_specs=[
            pl.BlockSpec((main, wide), lambda i: (0, 0), pipeline_mode=pl.Buffered(1)),
            pl.BlockSpec((main + tails, tile), lambda i: (0, jnp.minimum(i, first - 1))),
            pl.BlockSpec((tile, width), lambda i: (jnp.minimum(i, first - 1), 0)),
            pl.BlockSpec((fold, hid), lambda i: (jnp.maximum(i - first, 0), 0)),
        ],
        out_specs=pl.BlockSpec(memory_space=pl.ANY),
        out_shape=jax.ShapeDtypeStruct((main, wide + EXTRA), BF16),
        scratch_shapes=[
            pltpu.VMEM((tails, width), BF16),
            pltpu.VMEM((main + tails, hid), BF16),
            pltpu.VMEM((main + tails, 1), F32),
            pltpu.VMEM((2, main, fold), BF16),
            pltpu.VMEM((main, fold), BF16),
            pltpu.VMEM((main, fold), BF16),
            pltpu.VMEM((main, EXTRA), BF16),
            pltpu.SemaphoreType.DMA((4,)),
        ],
        compiler_params=pltpu.CompilerParams(vmem_limit_bytes=VMEM),
        cost_estimate=pl.CostEstimate(
            flops=4 * (main + tails) * width * hid, bytes_accessed=39_000_000, transcendentals=(main + tails) * hid
        ),
        name="back_and_pieces",
    )(rows, pre, w_down, w_up)


def combine_kernel(ids_ref, gate_ref, rows_ref, out_ref, grad_ref, acc_ref, sum_ref):
    step = pl.program_id(0)
    tok, width = out_ref.shape
    fold = width // QUARTERS
    ids = ids_ref[...]
    main, tail, quarter, spread, expert = picks(ids, step * GROUP)
    high = jnp.zeros(expert.shape, F32)
    low = jnp.zeros(expert.shape, F32)
    for slot in range(ids.shape[0]):
        same = expert == ids[slot : slot + 1, :]
        fixed = gate_ref[slot : slot + 1, :]
        high = high + jnp.where(same, (fixed // 256).astype(F32), 0.0)
        low = low + jnp.where(same, (fixed % 256).astype(F32), 0.0)
    high = dot(spread, high.astype(BF16)) * (1.0 / 256.0)
    low = dot(spread, low.astype(BF16)) * (1.0 / 65536.0)

    def weights(mask):
        return jnp.concatenate([jnp.where(mask, high, 0.0), jnp.where(mask, low, 0.0)], axis=1).astype(BF16)

    @pl.when(step == 0)
    def _():
        acc_ref[...] = jnp.zeros_like(acc_ref)
        sum_ref[...] = jnp.zeros_like(sum_ref)

    both = dot_tn(weights(main), rows_ref[:, :width])
    acc_ref[...] += both[:tok, :] + both[tok:, :]
    for q in range(QUARTERS):
        both = dot_tn(weights(jnp.logical_and(tail, quarter == q)), rows_ref[:, width : width + fold])
        acc_ref[:, q * fold : (q + 1) * fold] += both[:tok, :] + both[tok:, :]

    extra = rows_ref[:, width + fold :].astype(F32)
    value = jnp.where(main, extra[:, 0:1], 0.0) + jnp.where(
        jnp.logical_and(tail, quarter == 0), extra[:, EXTRA // 2 : EXTRA // 2 + 1], 0.0
    )
    value = dot_tn(spread, value.astype(BF16))
    for slot in range(ids.shape[0]):
        part = jnp.sum(jnp.where(expert == ids[slot : slot + 1, :], value, 0.0), axis=0, keepdims=True)
        sum_ref[slot : slot + 1, :] = sum_ref[slot : slot + 1, :] + part

    @pl.when(step == pl.num_programs(0) - 1)
    def _():
        out_ref[...] = acc_ref[...].astype(BF16)
        grad_ref[...] = sum_ref[...]


def combine(ids_t, gate_t, rows, width):
    top, tok = ids_t.shape
    main, wide = rows.shape
    size = GROUP * MAIN
    return pl.pallas_call(
        combine_kernel,
        grid=(main // size,),
        in_specs=[
            pl.BlockSpec((top, tok), lambda i: (0, 0)),
            pl.BlockSpec((top, tok), lambda i: (0, 0)),
            pl.BlockSpec((size, wide), lambda i: (i, 0)),
        ],
        out_specs=[
            pl.BlockSpec((tok, width), lambda i: (0, 0)),
            pl.BlockSpec((top, tok), lambda i: (0, 0)),
        ],
        out_shape=[
            jax.ShapeDtypeStruct((tok, width), BF16),
            jax.ShapeDtypeStruct((top, tok), F32),
        ],
        scratch_shapes=[pltpu.VMEM((tok, width), F32), pltpu.VMEM((top, tok), F32)],
        compiler_params=pltpu.CompilerParams(vmem_limit_bytes=VMEM),
        name="combine",
    )(ids_t, gate_t, rows)


def exchange(rows):
    experts = lax.axis_size("node") * lax.axis_size("local")
    wide = rows.shape[1]
    blocks = rows.reshape(experts, MAIN, wide)
    blocks = lax.all_to_all(blocks, ("node", "local"), split_axis=0, concat_axis=0, tiled=True)
    return blocks.reshape(experts * MAIN, wide)


def per_device(tokens, cotangent, expert_ids, gate_fixed, w_up, w_down):
    width = tokens.shape[1]
    ids_t = expert_ids.T
    gate_t = gate_fixed.T
    rows_x = exchange(send(ids_t, tokens))
    rows_dy = exchange(send(ids_t, cotangent))
    pre = pre_of(rows_x, w_up[0])
    pieces = pieces_of(rows_dy, pre, w_down[0], w_up[0])
    grad_input, grad_gate = combine(ids_t, gate_t, exchange(pieces), width)
    return grad_input, grad_gate.T.astype(BF16)


def solution(mesh):
    split = P(("node", "local"), None)
    experts = P(("node", "local"), None, None)
    return jax.shard_map(
        per_device,
        mesh=mesh,
        in_specs=(split, split, split, split, experts, experts),
        out_specs=(split, split),
        check_vma=False,
    )
```

time: 800 us -> 416 us (0.52)
  the two profiles are of different devices: /device:TPU:84 before, /device:TPU:1 now
where the time goes in v1:
time: 416 us; the launch traced here: 415 us
  waiting for transfers between devices  191 us (46%)
  blocking collectives  122 us (29%)
  Pallas kernels  74 us (18%)
  starting transfers between devices  25.4 us (6%)
    all_to_all x2, waiting for transfers between devices, exchange(): lax.all_to_all(blocks, ('node', 'local'), split_axis=0, concat_axis=0, ti...  191 us
    all_to_all x1, blocking collectives, exchange(): lax.all_to_all(blocks, ('node', 'local'), split_axis=0, concat_axis=0, ti...  122 us
    pallas_call x1, Pallas kernels, pieces_of(): pl.pallas_call(back_kernel, grid=(first + QUARTERS,), in_specs=[pl.BlockS...  32.2 us
    all_to_all x2, starting transfers between devices, exchange(): lax.all_to_all(blocks, ('node', 'local'), split_axis=0, concat_axis=0, ti...  25.4 us
    pallas_call x1, Pallas kernels, pre_of(): pl.pallas_call(pre_kernel, grid=(hid // tile,), in_specs=[pl.BlockSpec((m...  16.2 us
    pallas_call x2, Pallas kernels, send(): pl.pallas_call(send_kernel, grid=(experts // GROUP,), in_specs=[pl.BlockS...  16.2 us
    pallas_call x1, Pallas kernels, combine(): pl.pallas_call(combine_kernel, grid=(main // size,), in_specs=[pl.BlockSp...  9.37 us
  transfers between devices with their start and end apart: 2, of which 2 were waited for; matrix products, arithmetic and copies ran while one was open for 0% of the time, Pallas kernels for 6%

profile of v1, /device:TPU:1, one launch (start us, length us, event | category | flops | bytes accessed | tf_op | source)
XLA Modules:
  0.0 415.1 jit_solution(15267461465781953753)
XLA Ops:
  0.6 8.1 %pick_rows.3 = bf16[1024,4480]{1,0:T(8,128)(2,1)} custom-call(s32[8,128]{1,0:T(8,128)} %bitcast.16, bf16[128,3584]{1,0:T(8,128)(2,1)} %x_ref.3), custom_call_target="tpu_custom_call" | custom-call | flops 3758096384 | bytes 9175040 | tf_op jit(solution)/shard_map/pick_rows/pallas_call | solution.py:75
  8.7 11.9 %all-to-all-start.1 = ((bf16[128,8,4480]{2,1,0:T(8,128)(2,1)}), bf16[128,8,4480]{2,1,0:T(8,128)(2,1)}, u32[]{:S(2)}, u32[]{:S(2)}) async-start(bf16[128,8,4480]{2,1,0:T(8,128)(2,1)} %bitcast.15), calls=%async_computation.1 | async-start | bytes 18350080 | tf_op jit(solution)/shard_map/all_to_all | solution.py:337
  20.6 8.1 %pick_rows.2 = bf16[1024,4480]{1,0:T(8,128)(2,1)} custom-call(s32[8,128]{1,0:T(8,128)} %bitcast.17, bf16[128,3584]{1,0:T(8,128)(2,1)} %x_ref.2), custom_call_target="tpu_custom_call" | custom-call | flops 3758096384 | bytes 9175040 | tf_op jit(solution)/shard_map/pick_rows/pallas_call | solution.py:75
  28.7 99.8 %all-to-all-done.1 = bf16[128,8,4480]{2,1,0:T(8,128)(2,1)} async-done(((bf16[128,8,4480]{2,1,0:T(8,128)(2,1)}), bf16[128,8,4480]{2,1,0:T(8,128)(2,1)}, u32[]{:S(2)}, u32[]{:S(2)}) %all-to-all-start.1) | async-done | bytes 9175072 | tf_op jit(solution)/shard_map/all_to_all | solution.py:337
  128.5 13.5 %all-to-all-start = ((bf16[128,8,4480]{2,1,0:T(8,128)(2,1)}), bf16[128,8,4480]{2,1,0:T(8,128)(2,1)}, u32[]{:S(2)}, u32[]{:S(2)}) async-start(bf16[128,8,4480]{2,1,0:T(8,128)(2,1)} %bitcast.14), calls=%async_computation | async-start | bytes 18350080 | tf_op jit(solution)/shard_map/all_to_all | solution.py:337
  142.0 16.2 %pre.1.pre_ref = f32[1280,1024]{1,0:T(8,128)} custom-call(bf16[1024,4480]{1,0:T(8,128)(2,1)} %bitcast.5.rows_ref, bf16[3584,1024]{1,0:T(8,128)(2,1)} %bitcast.20), custom_call_target="tpu_custom_call" | custom-call | flops 9395240960 | bytes 22000000 | tf_op jit(solution)/shard_map/pre/pallas_call | solution.py:121
  158.2 91.6 %all-to-all-done = bf16[128,8,4480]{2,1,0:T(8,128)(2,1)} async-done(((bf16[128,8,4480]{2,1,0:T(8,128)(2,1)}), bf16[128,8,4480]{2,1,0:T(8,128)(2,1)}, u32[]{:S(2)}, u32[]{:S(2)}) %all-to-all-start) | async-done | bytes 9175072 | tf_op jit(solution)/shard_map/all_to_all | solution.py:337
  249.8 32.2 %back_and_pieces.1 = bf16[1024,4608]{1,0:T(8,128)(2,1)} custom-call(bf16[1024,4480]{1,0:T(8,128)(2,1)} %bitcast.3.rows_ref, f32[1280,1024]{1,0:T(8,128)} %pre.1.pre_ref, bf16[1024,3584]{1,0:T(8,128)(2,1)} %bitcast.22, bf16[3584,1024]{1,0:T(8,128)(2,1)} %bitcast.21), custom_call_target="tpu_custom_call" | custom-call | flops 18790481920 | bytes 39000000 | tf_op jit(solution)/shard_map/back_and_pieces/pallas_call | solution.py:233
  282.1 122.4 %all_to_all.15 = bf16[128,8,4608]{2,1,0:T(8,128)(2,1)} all-to-all(bf16[128,8,4608]{2,1,0:T(8,128)(2,1)} %bitcast.13), channel_id=1, replica_groups=mesh['node'=16,'local'=8] {'node','local'}, dimensions={0} | all-to-all | bytes 18874368 | tf_op jit(solution)/shard_map/all_to_all | solution.py:337
  404.5 9.4 %combine.1 = (bf16[128,3584]{1,0:T(8,128)(2,1)}, f32[8,128]{1,0:T(8,128)}) custom-call(s32[8,128]{1,0:T(8,128)} %bitcast.18, s32[8,128]{1,0:T(8,128)} %bitcast.19, bf16[1024,4608]{1,0:T(8,128)(2,1)} %bitcast.12), custom_call_target="tpu_custom_call" | custom-call | tf_op jit(solution)/shard_map/combine/pallas_call | solution.py:311
  413.8 1.3 convert_bitcast_fusion
Async XLA Ops:
  8.7 119.8 %all-to-all-start.1 = ((bf16[128,8,4480]{2,1,0:T(8,128)(2,1)}), bf16[128,8,4480]{2,1,0:T(8,128)(2,1)}, u32[]{:S(2)}, u32[]{:S(2)}) async-start(bf16[128,8,4480]{2,1,0:T(8,128)(2,1)} %bitcast.15), calls=%async_computation.1 | async-start | bytes 18350080 | tf_op jit(solution)/shard_map/all_to_all | solution.py:337
  128.5 121.3 %all-to-all-start = ((bf16[128,8,4480]{2,1,0:T(8,128)(2,1)}), bf16[128,8,4480]{2,1,0:T(8,128)(2,1)}, u32[]{:S(2)}, u32[]{:S(2)}) async-start(bf16[128,8,4480]{2,1,0:T(8,128)(2,1)} %bitcast.14), calls=%async_computation | async-start | bytes 18350080 | tf_op jit(solution)/shard_map/all_to_all | solution.py:337

commit v2 on v1

v2 whole, which is shorter than its diff:
```python
import functools

import jax
import jax.numpy as jnp
from jax import lax
from jax.experimental import pallas as pl
from jax.experimental.pallas import tpu as pltpu
from jax.sharding import PartitionSpec as P

TOP = 8
NODES_MAX = 4
CAP = 10
MAIN = 8
QUARTERS = 4
GROUP = 32
EXTRA = 128
VMEM = 56 * 1024 * 1024
BF16 = jnp.bfloat16
F32 = jnp.float32


def iota(shape, dim):
    return lax.broadcasted_iota(jnp.int32, shape, dim)


def dot(a, b):
    return jnp.dot(a, b, preferred_element_type=F32)


def dot_nt(a, b):
    return lax.dot_general(a, b, (((1,), (1,)), ((), ())), preferred_element_type=F32)


def dot_tn(a, b):
    return lax.dot_general(a, b, (((0,), (0,)), ((), ())), preferred_element_type=F32)


def slots_of(ids, first):
    tok = ids.shape[1]
    expert = first + iota((GROUP, tok), 0)
    hit = jnp.zeros((GROUP, tok), F32)
    for slot in range(ids.shape[0]):
        hit = hit + (expert == ids[slot : slot + 1, :]).astype(F32)
    earlier = (iota((tok, tok), 0) < iota((tok, tok), 1)).astype(BF16)
    before = dot(hit.astype(BF16), earlier)
    place = jnp.where(hit > 0.5, before, -1.0)
    rows = GROUP * MAIN
    spread = (iota((rows, GROUP), 0) // MAIN == iota((rows, GROUP), 1)).astype(BF16)
    return dot(spread, place.astype(BF16)), spread, expert


def picks(ids, first):
    place, spread, expert = slots_of(ids, first)
    row = iota(place.shape, 0)
    main = place == (row % MAIN).astype(F32)
    tail = place == (MAIN + row % 2).astype(F32)
    quarter = (row % MAIN) // 2
    return main, tail, quarter, spread, expert


def places(ids, first, count):
    tok = ids.shape[1]
    expert = first + iota((count, tok), 0)
    hit = jnp.zeros((count, tok), F32)
    for slot in range(ids.shape[0]):
        hit = hit + (expert == ids[slot : slot + 1, :]).astype(F32)
    earlier = (iota((tok, tok), 0) < iota((tok, tok), 1)).astype(BF16)
    return jnp.where(hit > 0.5, dot(hit.astype(BF16), earlier), -1.0), expert


def node_kernel(ids_ref, x_ref, out_ref, *, share, nodes, local):
    width = x_ref.shape[1]
    tok = x_ref.shape[0]
    rows = out_ref.shape[0]
    some = rows // share
    ids = ids_ref[...]
    first = pl.program_id(0) * some
    node = first + iota((some, tok), 0)
    named = jnp.zeros((some, tok), F32)
    for slot in range(ids.shape[0]):
        named = jnp.maximum(named, (node == ids[slot : slot + 1, :] // local).astype(F32))
    earlier = (iota((tok, tok), 0) < iota((tok, tok), 1)).astype(BF16)
    rank = jnp.where(named > 0.5, dot(named.astype(BF16), earlier), -1.0)
    spread = (iota((rows, some), 0) // share == iota((rows, some), 1)).astype(BF16)
    wanted = (iota((rows, tok), 0) % share).astype(F32)
    pick = (dot(spread, rank.astype(BF16)) == wanted).astype(BF16)
    out_ref[:, :width] = dot(pick, x_ref[...]).astype(BF16)
    count = some * local
    place, _ = places(ids, first * local, count)
    slots = dot_nt(pick, place.astype(BF16))
    slots = jnp.where(iota((rows, count), 0) // share == iota((rows, count), 1) // local, slots, 0.0)
    lanes = (iota((count, EXTRA), 0) % local == iota((count, EXTRA), 1)).astype(BF16)
    out_ref[:, width:] = dot(slots.astype(BF16), lanes).astype(BF16)


def node_rows(ids_t, x, nodes, local):
    top, tok = ids_t.shape
    width = x.shape[1]
    share = tok * NODES_MAX // nodes
    steps = 4
    return pl.pallas_call(
        functools.partial(node_kernel, share=share, nodes=nodes, local=local),
        grid=(steps,),
        in_specs=[
            pl.BlockSpec((top, tok), lambda i: (0, 0)),
            pl.BlockSpec((tok, width), lambda i: (0, 0)),
        ],
        out_specs=pl.BlockSpec((nodes * share // steps, width + EXTRA), lambda i: (i, 0)),
        out_shape=jax.ShapeDtypeStruct((nodes * share, width + EXTRA), BF16),
        compiler_params=pltpu.CompilerParams(vmem_limit_bytes=VMEM),
        cost_estimate=pl.CostEstimate(
            flops=2 * nodes * share * 256 * width, bytes_accessed=5_000_000, transcendentals=0
        ),
        name="node_rows",
    )(ids_t, x)


def part_kernel(me_ref, rows_ref, slots_ref, *refs, share, nodes, local):
    outs, (main_ref, tail_ref) = refs[:local], refs[local:]
    x, c = me_ref[0] // 2, me_ref[0] % 2
    half = nodes // 2
    rows = half * share
    mains = half * MAIN
    tails = 2 * nodes

    def to_of(rel):
        return ((x + rel // 2) % (local // 2)) * 2 + (c + rel) % 2

    @pl.when(pl.program_id(0) == 0)
    def _():
        col, lane = iota((local * mains, EXTRA), 0), iota((local * mains, EXTRA), 1)
        spread = (lane == to_of(col // mains)).astype(BF16)
        shape = (local * mains, rows)
        row, at = iota(shape, 0), iota(shape, 1)
        fits = at // share == (row % mains) // MAIN
        slot = (row % MAIN).astype(F32)
        for g in range(2):
            place = dot_nt(spread, slots_ref[g * rows : (g + 1) * rows, :])
            main_ref[g] = jnp.logical_and(place == slot, fits).astype(BF16)
        col, lane = iota((local * tails, EXTRA), 0), iota((local * tails, EXTRA), 1)
        spread = (lane == to_of(col // tails)).astype(BF16)
        shape = (local * tails, 2 * rows)
        row, at = iota(shape, 0), iota(shape, 1)
        place = dot_nt(spread, slots_ref[...])
        fits = at // share == (row % tails) // 2
        tail_ref[...] = jnp.logical_and(place == (MAIN + row % 2).astype(F32), fits).astype(BF16)

    for g in range(2):
        got = dot(main_ref[g], rows_ref[g * rows : (g + 1) * rows, :]).astype(BF16)
        for rel in range(local):
            outs[rel][g * mains : (g + 1) * mains, :] = got[rel * mains : (rel + 1) * mains, :]
    got = dot(tail_ref[...], rows_ref[...]).astype(BF16)
    for rel in range(local):
        outs[rel][2 * mains :, :] = got[rel * tails : (rel + 1) * tails, :]


def part_rows(me, rows, nodes, local):
    total, wide = rows.shape
    width = wide - EXTRA
    share = total // nodes
    fold = width // QUARTERS
    size = nodes * CAP
    return pl.pallas_call(
        functools.partial(part_kernel, share=share, nodes=nodes, local=local),
        grid=(QUARTERS,),
        in_specs=[
            pl.BlockSpec(memory_space=pltpu.SMEM),
            pl.BlockSpec((total, fold), lambda i: (0, i)),
            pl.BlockSpec((total, EXTRA), lambda i: (0, width // EXTRA)),
        ],
        out_specs=[pl.BlockSpec((size, fold), lambda i: (0, i)) for _ in range(local)],
        out_shape=[jax.ShapeDtypeStruct((size, width), BF16) for _ in range(local)],
        scratch_shapes=[
            pltpu.VMEM((2, local * nodes // 2 * MAIN, total // 2), BF16),
            pltpu.VMEM((local * nodes * 2, total), BF16),
        ],
        compiler_params=pltpu.CompilerParams(vmem_limit_bytes=VMEM),
        cost_estimate=pl.CostEstimate(
            flops=4 * local * size * 256 * width, bytes_accessed=13_000_000, transcendentals=0
        ),
        name="part_rows",
    )(me, rows, rows)


def gathered_kernel(me_ref, rows_ref, ids_ref, out_ref, main_ref, tail_ref, *, tok, nodes, local):
    x, c = me_ref[0] // 2, me_ref[0] % 2
    chips = local // 2
    both = 2 * tok
    pair = 2 * MAIN
    per_node = local * CAP

    def chip_at(d):
        return (x + chips - d) % chips

    @pl.when(pl.program_id(0) == 0)
    def _():
        lane = iota((tok, EXTRA), 1)
        earlier = (iota((tok, tok), 1) < iota((tok, tok), 0)).astype(BF16)

        def place_of(source):
            ids = ids_ref[pl.ds(source * tok, tok), :].astype(F32)
            hit = jnp.zeros((tok, EXTRA), F32)
            for slot in range(TOP):
                hit = hit + (ids[:, slot : slot + 1] == (lane * local + me_ref[0]).astype(F32)).astype(F32)
            return jnp.where(hit > 0.5, dot(earlier, hit.astype(BF16)), -1.0).astype(BF16)

        shape = (nodes * pair, EXTRA)
        spread = (iota(shape, 0) // pair == iota(shape, 1)).astype(BF16)
        shape = (nodes * pair, both)
        row, at = iota(shape, 0), iota(shape, 1)
        core = at // tok
        main_fits = core == ((row % pair) // MAIN + c) % 2
        main_slot = (row % MAIN).astype(F32)
        tail_fits = core == ((row % pair) // 2 % 2 + c) % 2
        tail_slot = (MAIN + row % 2).astype(F32)
        for d in range(chips):
            a = chip_at(d)
            place = jnp.concatenate([place_of(2 * a), place_of(2 * a + 1)], axis=0)
            place = dot_nt(spread, place)
            main_ref[d] = jnp.logical_and(place == main_slot, main_fits).astype(BF16)
            here = jnp.logical_and(tail_fits, (row % pair) // 4 == d)
            tail_ref[d] = jnp.logical_and(place == tail_slot, here).astype(BF16)

    tail = None
    for d in range(chips):
        rows = rows_ref[pl.ds(pl.multiple_of(chip_at(d) * both, both), both), :]
        got = dot(main_ref[d], rows).astype(BF16)
        for n in range(nodes):
            out_ref[n * per_node + d * pair : n * per_node + (d + 1) * pair, :] = got[n * pair : (n + 1) * pair, :]
        part = dot(tail_ref[d], rows)
        tail = part if tail is None else tail + part
    tail = tail.astype(BF16)
    for n in range(nodes):
        out_ref[n * per_node + local * MAIN : (n + 1) * per_node, :] = tail[n * pair : (n + 1) * pair, :]


def gathered_rows(me, rows, nodes, local):
    total, wide = rows.shape
    width = wide - EXTRA
    tok = total // local
    fold = width // QUARTERS
    size = nodes * local * CAP
    pair = 2 * MAIN
    return pl.pallas_call(
        functools.partial(gathered_kernel, tok=tok, nodes=nodes, local=local),
        grid=(QUARTERS,),
        in_specs=[
            pl.BlockSpec(memory_space=pltpu.SMEM),
            pl.BlockSpec((total, fold), lambda i: (0, i)),
            pl.BlockSpec((total, EXTRA), lambda i: (0, width // EXTRA)),
        ],
        out_specs=pl.BlockSpec((size, fold), lambda i: (0, i)),
        out_shape=jax.ShapeDtypeStruct((size, width), BF16),
        scratch_shapes=[
            pltpu.VMEM((local // 2, nodes * pair, 2 * tok), BF16),
            pltpu.VMEM((local // 2, nodes * pair, 2 * tok), BF16),
        ],
        compiler_params=pltpu.CompilerParams(vmem_limit_bytes=VMEM),
        cost_estimate=pl.CostEstimate(
            flops=4 * size * 256 * width, bytes_accessed=17_000_000, transcendentals=0
        ),
        name="gathered_rows",
    )(me, rows, rows)


def pre_kernel(*refs, nodes, local):
    rows_refs, (w_ref, out_ref, rows_ref, made_ref, sems) = refs[:local], refs[local:]
    size = nodes * CAP
    per_node = local * CAP

    @pl.when(pl.program_id(0) == 0)
    def _():
        copies = [
            pltpu.make_async_copy(rows_refs[rel], rows_ref.at[pl.ds(rel * size, size), :], sems.at[rel])
            for rel in range(local)
        ]
        for copy in copies:
            copy.start()
        for copy in copies:
            copy.wait()

    made_ref[...] = dot(rows_ref[...], w_ref[...])
    for n in range(nodes):
        for rel in range(local):
            to, at = n * per_node + rel * MAIN, rel * size + n * MAIN
            out_ref[to : to + MAIN, :] = made_ref[at : at + MAIN, :]
            to, at = n * per_node + local * MAIN + rel * 2, rel * size + nodes * MAIN + n * 2
            out_ref[to : to + 2, :] = made_ref[at : at + 2, :]


def pre_of(parts, w_up, nodes, local, tile=256):
    width, hid = w_up.shape
    total = nodes * local * CAP
    return pl.pallas_call(
        functools.partial(pre_kernel, nodes=nodes, local=local),
        grid=(hid // tile,),
        in_specs=[pl.BlockSpec(memory_space=pl.ANY)] * local + [pl.BlockSpec((width, tile), lambda i: (0, i))],
        out_specs=pl.BlockSpec((total, tile), lambda i: (0, i)),
        out_shape=jax.ShapeDtypeStruct((total, hid), F32),
        scratch_shapes=[
            pltpu.VMEM((total, width), BF16),
            pltpu.VMEM((total, tile), F32),
            pltpu.SemaphoreType.DMA((local,)),
        ],
        compiler_params=pltpu.CompilerParams(vmem_limit_bytes=VMEM),
        cost_estimate=pl.CostEstimate(
            flops=2 * total * width * hid, bytes_accessed=22_000_000, transcendentals=0
        ),
        name="pre",
    )(*parts, w_up)


def back_kernel(
    me_ref, rows_ref, pre_ref, down_ref, up_ref, out_ref, raw_ref, inner_ref, gate_ref, piece_ref, stack_ref, fold_ref, extra_ref, sems, *, local
):
    step = pl.program_id(0)
    width = down_ref.shape[1]
    tile = down_ref.shape[0]
    hid = inner_ref.shape[1]
    main = out_ref.shape[0]
    fold = width // QUARTERS
    tails = 2 * GROUP
    size = GROUP * MAIN
    groups = main // size
    first = hid // tile

    for j in range(first):

        @pl.when(step == j)
        def _():
            pre = pre_ref[...]
            back = dot_nt(rows_ref[...], down_ref[...])
            sig = 1.0 / (1.0 + jnp.exp(-pre))
            act = (pre * sig).astype(BF16).astype(F32)
            raw_ref[:, j * tile : (j + 1) * tile] = (back * sig * (1.0 + pre * (1.0 - sig))).astype(BF16)
            gate = jnp.sum(act * back, axis=-1, keepdims=True)
            gate_ref[...] = gate if j == 0 else gate_ref[...] + gate

    def return_order():
        x, c = me_ref[0] // 2, me_ref[0] % 2
        rows = size + tails
        to, at = iota((rows, rows), 0), iota((rows, rows), 1)
        is_main = to < size
        source = jnp.where(is_main, to // MAIN, (to - size) // 2)
        node, place = source // local, source % local
        rel = ((x + local // 2 - place // 2) % (local // 2)) * 2 + (place + c) % 2
        start = jnp.where(is_main, rel * MAIN + to % MAIN, local * MAIN + rel * 2 + to % 2)
        return (at == node * (local * CAP) + start).astype(BF16)

    def copy_of(q):
        return pltpu.make_async_copy(
            piece_ref.at[q % 2], out_ref.at[:, pl.ds(q * fold, fold)], sems.at[q % 2]
        )

    fold_copy = pltpu.make_async_copy(fold_ref, out_ref.at[:, pl.ds(width, fold)], sems.at[2])
    extra_copy = pltpu.make_async_copy(extra_ref, out_ref.at[:, pl.ds(width + fold, EXTRA)], sems.at[3])

    for q in range(QUARTERS):

        @pl.when(step == first + q)
        def _():
            if q == 0:
                order = return_order()
                rows = size + tails
                for b in range(groups):
                    got = dot(order, raw_ref[b * rows : (b + 1) * rows, :]).astype(BF16)
                    inner_ref[b * size : (b + 1) * size, :] = got[:size, :]
                    inner_ref[main + b * tails : main + (b + 1) * tails, :] = got[size:, :]
            if q >= 2:
                copy_of(q - 2).wait()
            piece_ref[q % 2] = dot_nt(inner_ref[:main, :], up_ref[...]).astype(BF16)
            copy_of(q).start()
            if q == 0:
                pick = (iota((size, tails), 0) // MAIN == iota((size, tails), 1) // 2).astype(BF16)
                parity = iota((size, EXTRA), 0) % 2
                low = iota((size, EXTRA), 1) < EXTRA // 2
                for b in range(groups):
                    gates = jnp.broadcast_to(gate_ref[b * rows : (b + 1) * rows, :], (rows, EXTRA))
                    gates = dot(order, gates.astype(BF16))
                    mains, last = gates[:size, :], gates[size:, :]
                    odd = (iota((tails, EXTRA), 0) % 2 == 1)
                    even_rows = dot(pick, jnp.where(odd, 0.0, last).astype(BF16))
                    odd_rows = dot(pick, jnp.where(odd, last, 0.0).astype(BF16))
                    tail_rows = jnp.where(parity == 1, odd_rows, even_rows)
                    extra_ref[b * size : (b + 1) * size, :] = jnp.where(
                        low, mains, tail_rows
                    ).astype(BF16)
                extra_copy.start()
            piece = dot_nt(inner_ref[main:, :], up_ref[...]).astype(BF16)
            for b in range(groups):
                stack_ref[b * size + q * tails : b * size + (q + 1) * tails, :] = piece[b * tails : (b + 1) * tails, :]
            if q == QUARTERS - 1:
                to = iota((size, size), 0)
                source = ((to % MAIN) // 2) * tails + (to // MAIN) * 2 + to % 2
                order = (source == iota((size, size), 1)).astype(BF16)
                for b in range(groups):
                    fold_ref[b * size : (b + 1) * size, :] = dot(
                        order, stack_ref[b * size : (b + 1) * size, :]
                    ).astype(BF16)
                fold_copy.start()
                copy_of(q - 1).wait()
                copy_of(q).wait()
                extra_copy.wait()
                fold_copy.wait()


def pieces_of(me, rows, pre, w_down, w_up, local, tile=256):
    total, width = rows.shape
    hid = w_down.shape[0]
    main = total // CAP * MAIN
    fold = width // QUARTERS
    first = hid // tile
    return pl.pallas_call(
        functools.partial(back_kernel, local=local),
        grid=(first + QUARTERS,),
        in_specs=[
            pl.BlockSpec(memory_space=pltpu.SMEM),
            pl.BlockSpec((total, width), lambda i: (0, 0), pipeline_mode=pl.Buffered(1)),
            pl.BlockSpec((total, tile), lambda i: (0, jnp.minimum(i, first - 1))),
            pl.BlockSpec((tile, width), lambda i: (jnp.minimum(i, first - 1), 0)),
            pl.BlockSpec((fold, hid), lambda i: (jnp.maximum(i - first, 0), 0)),
        ],
        out_specs=pl.BlockSpec(memory_space=pl.ANY),
        out_shape=jax.ShapeDtypeStruct((main, width + fold + EXTRA), BF16),
        scratch_shapes=[
            pltpu.VMEM((total, hid), BF16),
            pltpu.VMEM((total, hid), BF16),
            pltpu.VMEM((total, 1), F32),
            pltpu.VMEM((2, main, fold), BF16),
            pltpu.VMEM((main, fold), BF16),
            pltpu.VMEM((main, fold), BF16),
            pltpu.VMEM((main, EXTRA), BF16),
            pltpu.SemaphoreType.DMA((4,)),
        ],
        compiler_params=pltpu.CompilerParams(vmem_limit_bytes=VMEM),
        cost_estimate=pl.CostEstimate(
            flops=4 * total * width * hid, bytes_accessed=39_000_000, transcendentals=total * hid
        ),
        name="back_and_pieces",
    )(me, rows, pre, w_down, w_up)


def combine_kernel(ids_ref, gate_ref, rows_ref, out_ref, grad_ref, acc_ref, sum_ref):
    step = pl.program_id(0)
    tok, width = out_ref.shape
    fold = width // QUARTERS
    ids = ids_ref[...]
    main, tail, quarter, spread, expert = picks(ids, step * GROUP)
    high = jnp.zeros(expert.shape, F32)
    low = jnp.zeros(expert.shape, F32)
    for slot in range(ids.shape[0]):
        same = expert == ids[slot : slot + 1, :]
        fixed = gate_ref[slot : slot + 1, :]
        high = high + jnp.where(same, (fixed // 256).astype(F32), 0.0)
        low = low + jnp.where(same, (fixed % 256).astype(F32), 0.0)
    high = dot(spread, high.astype(BF16)) * (1.0 / 256.0)
    low = dot(spread, low.astype(BF16)) * (1.0 / 65536.0)

    def weights(mask):
        return jnp.concatenate([jnp.where(mask, high, 0.0), jnp.where(mask, low, 0.0)], axis=1).astype(BF16)

    @pl.when(step == 0)
    def _():
        acc_ref[...] = jnp.zeros_like(acc_ref)
        sum_ref[...] = jnp.zeros_like(sum_ref)

    both = dot_tn(weights(main), rows_ref[:, :width])
    acc_ref[...] += both[:tok, :] + both[tok:, :]
    for q in range(QUARTERS):
        both = dot_tn(weights(jnp.logical_and(tail, quarter == q)), rows_ref[:, width : width + fold])
        acc_ref[:, q * fold : (q + 1) * fold] += both[:tok, :] + both[tok:, :]

    extra = rows_ref[:, width + fold :].astype(F32)
    value = jnp.where(main, extra[:, 0:1], 0.0) + jnp.where(
        jnp.logical_and(tail, quarter == 0), extra[:, EXTRA // 2 : EXTRA // 2 + 1], 0.0
    )
    value = dot_tn(spread, value.astype(BF16))
    for slot in range(ids.shape[0]):
        part = jnp.sum(jnp.where(expert == ids[slot : slot + 1, :], value, 0.0), axis=0, keepdims=True)
        sum_ref[slot : slot + 1, :] = sum_ref[slot : slot + 1, :] + part

    @pl.when(step == pl.num_programs(0) - 1)
    def _():
        out_ref[...] = acc_ref[...].astype(BF16)
        grad_ref[...] = sum_ref[...]


def combine(ids_t, gate_t, rows, width):
    top, tok = ids_t.shape
    main, wide = rows.shape
    size = GROUP * MAIN
    return pl.pallas_call(
        combine_kernel,
        grid=(main // size,),
        in_specs=[
            pl.BlockSpec((top, tok), lambda i: (0, 0)),
            pl.BlockSpec((top, tok), lambda i: (0, 0)),
            pl.BlockSpec((size, wide), lambda i: (i, 0)),
        ],
        out_specs=[
            pl.BlockSpec((tok, width), lambda i: (0, 0)),
            pl.BlockSpec((top, tok), lambda i: (0, 0)),
        ],
        out_shape=[
            jax.ShapeDtypeStruct((tok, width), BF16),
            jax.ShapeDtypeStruct((top, tok), F32),
        ],
        scratch_shapes=[pltpu.VMEM((tok, width), F32), pltpu.VMEM((top, tok), F32)],
        compiler_params=pltpu.CompilerParams(vmem_limit_bytes=VMEM),
        name="combine",
    )(ids_t, gate_t, rows)


def exchange(rows, axes):
    count = lax.axis_size(axes)
    blocks = rows.reshape(count, rows.shape[0] // count, rows.shape[1])
    blocks = lax.all_to_all(blocks, axes, split_axis=0, concat_axis=0, tiled=True)
    return blocks.reshape(rows.shape)


def shift(rows, rel, local):
    chips = local // 2
    pairs = [(2 * x + c, 2 * ((x + rel // 2) % chips) + (c + rel) % 2) for x in range(chips) for c in range(2)]
    return lax.ppermute(rows, "local", pairs)


def per_device(tokens, cotangent, expert_ids, gate_fixed, w_up, w_down):
    nodes, local = lax.axis_size("node"), lax.axis_size("local")
    width = tokens.shape[1]
    ids_t = expert_ids.T
    gate_t = gate_fixed.T
    me = lax.axis_index("local").astype(jnp.int32).reshape(1)
    marked = jnp.concatenate(
        [cotangent, jnp.pad(expert_ids.astype(BF16), ((0, 0), (0, EXTRA - expert_ids.shape[1])))], axis=1
    )
    rows_dy = lax.all_gather(marked, "local", tiled=True)
    rows_x = exchange(node_rows(ids_t, tokens, nodes, local), "node")
    rows_dy = exchange(gathered_rows(me, rows_dy, nodes, local), "node")
    parts = part_rows(me, rows_x, nodes, local)
    parts = [parts[0]] + [shift(parts[rel], rel, local) for rel in range(1, local)]
    pre = pre_of(parts, w_up[0], nodes, local)
    pieces = pieces_of(me, rows_dy, pre, w_down[0], w_up[0], local)
    grad_input, grad_gate = combine(ids_t, gate_t, exchange(pieces, ("node", "local")), width)
    return grad_input, grad_gate.T.astype(BF16)


def solution(mesh):
    split = P(("node", "local"), None)
    experts = P(("node", "local"), None, None)
    return jax.shard_map(
        per_device,
        mesh=mesh,
        in_specs=(split, split, split, split, experts, experts),
        out_specs=(split, split),
        check_vma=False,
    )
```

time: 416 us -> 391 us (0.940)
  waiting for transfers between devices: 191 us -> 141 us
  between operations: 0.66 us -> 14.1 us
  Pallas kernels: 74 us -> 85.8 us
    all_to_all x2, waiting for transfers between devices: 191 us -> 10 us  [exchange(): lax.all_to_all(blocks, axes, split_axis=0, concat_axis=0, tiled=True)]
    ppermute x0 -> x7, waiting for transfers between devices: none -> 94.9 us  [shift(): return lax.ppermute(rows, 'local', pairs)]
    all_gather x0 -> x1, waiting for transfers between devices: none -> 35.6 us  [per_device(): rows_dy = lax.all_gather(marked, 'local', tiled=True)]
    all_to_all x2, starting transfers between devices: 25.4 us -> 13.4 us  [exchange(): lax.all_to_all(blocks, axes, split_axis=0, concat_axis=0, tiled=True)]
    pallas_call x4 -> x5, Pallas kernels: 64.6 us -> 76.4 us  [the longest x1 34.5 us: pieces_of(): pl.pallas_call(functools.partial(back_kernel, local=local), grid=(first +...]
    ppermute x0 -> x7, starting transfers between devices: none -> 11.5 us  [shift(): return lax.ppermute(rows, 'local', pairs)]
  transfers between devices with their start and end apart: 2 -> 10, of which waited for: 2 -> 7; matrix products, arithmetic and copies ran while one was open for 0% -> 0% of each run, Pallas kernels for 6% -> 11%
where the time goes in v2:
time: 391 us; the launch traced here: 390 us
  waiting for transfers between devices  141 us (36%)
  blocking collectives  119 us (30%)
  Pallas kernels  85.8 us (22%)
  starting transfers between devices  25 us (6%)
  between operations  14.1 us (4%)
  other arithmetic  4.14 us (1%)
    all_to_all x1, blocking collectives, exchange(): lax.all_to_all(blocks, axes, split_axis=0, concat_axis=0, tiled=True)  119 us
    ppermute x7, waiting for transfers between devices, shift(): return lax.ppermute(rows, 'local', pairs)  94.9 us
    all_gather x1, waiting for transfers between devices, per_device(): rows_dy = lax.all_gather(marked, 'local', tiled=True)  35.6 us
    pallas_call x1, Pallas kernels, pieces_of(): pl.pallas_call(functools.partial(back_kernel, local=local), grid=(first +...  34.5 us
    pallas_call x1, Pallas kernels, pre_of(): pl.pallas_call(functools.partial(pre_kernel, nodes=nodes, local=local), g...  16.9 us
    all_to_all x2, starting transfers between devices, exchange(): lax.all_to_all(blocks, axes, split_axis=0, concat_axis=0, tiled=True)  13.4 us
    ppermute x7, starting transfers between devices, shift(): return lax.ppermute(rows, 'local', pairs)  11.5 us
    pallas_call x1, Pallas kernels, gathered_rows(): pl.pallas_call(functools.partial(gathered_kernel, tok=tok, nodes=nodes, l...  10.8 us
  transfers between devices with their start and end apart: 10, of which 7 were waited for; matrix products, arithmetic and copies ran while one was open for 0% of the time, Pallas kernels for 11%

profile of v2, /device:TPU:1, one launch (start us, length us, event | category | flops | bytes accessed | tf_op | source)
XLA Modules:
  0.0 390.0 jit_solution(7888020610139678821)
XLA Ops:
  8.0 2.2 fusion.1
  10.2 5.9 %node_rows.1 = bf16[512,3712]{1,0:T(8,128)(2,1)} custom-call(s32[8,128]{1,0:T(8,128)} %bitcast.17, bf16[128,3584]{1,0:T(8,128)(2,1)} %x_ref.1), custom_call_target="tpu_custom_call" | custom-call | flops 939524096 | bytes 5000000 | tf_op jit(solution)/shard_map/node_rows/pallas_call | solution.py:101
  16.1 8.6 %all-to-all-start.1 = ((bf16[16,32,3712]{2,1,0:T(8,128)(2,1)}), bf16[16,32,3712]{2,1,0:T(8,128)(2,1)}, u32[]{:S(2)}, u32[]{:S(2)}) async-start(bf16[16,32,3712]{2,1,0:T(8,128)(2,1)} %bitcast.15), calls=%async_computation.1 | async-start | bytes 7602176 | tf_op jit(solution)/shard_map/all_to_all | solution.py:517
  24.8 35.6 %all-gather.2.cloned.1.call-done.rows_ref.ids_ref = bf16[1024,3712]{1,0:T(8,128)(2,1)} async-done(((bf16[128,3712]{1,0:T(8,128)(2,1)}), bf16[1024,3712]{1,0:T(8,128)(2,1)}) %all-gather.2.cloned.1.call-update) | async-done | bytes 7602192 | tf_op jit(solution)/shard_map/all_gather | solution.py:536
  60.4 10.8 %gathered_rows.1 = bf16[1280,3584]{1,0:T(8,128)(2,1)} custom-call(s32[1]{0:T(128)} %bitcast.2.me_ref, bf16[1024,3712]{1,0:T(8,128)(2,1)} %all-gather.2.cloned.1.call-done.rows_ref.ids_ref, bf16[1024,3712]{1,0:T(8,128)(2,1)} %all-gather.2.cloned.1.call-done.rows_ref.ids_ref), custom_call_target="tpu_custom_call" | custom-call | flops 4697620480 | bytes 17000000 | tf_op jit(solution)/shard_map/gathered_rows/pallas_call | solution.py:244
  71.2 10.0 %all-to-all-done.1 = bf16[16,32,3712]{2,1,0:T(8,128)(2,1)} async-done(((bf16[16,32,3712]{2,1,0:T(8,128)(2,1)}), bf16[16,32,3712]{2,1,0:T(8,128)(2,1)}, u32[]{:S(2)}, u32[]{:S(2)}) %all-to-all-start.1) | async-done | bytes 3801120 | tf_op jit(solution)/shard_map/all_to_all | solution.py:517
  81.2 4.8 %all-to-all-start = ((bf16[16,80,3584]{2,1,0:T(8,128)(2,1)}), bf16[16,80,3584]{2,1,0:T(8,128)(2,1)}, u32[]{:S(2)}, u32[]{:S(2)}) async-start(bf16[16,80,3584]{2,1,0:T(8,128)(2,1)} %bitcast.14), calls=%async_computation | async-start | bytes 18350080 | tf_op jit(solution)/shard_map/all_to_all | solution.py:517
  86.0 8.4 %part_rows.1 = (bf16[160,3584]{1,0:T(8,128)(2,1)}, bf16[160,3584]{1,0:T(8,128)(2,1)}, bf16[160,3584]{1,0:T(8,128)(2,1)}, bf16[160,3584]{1,0:T(8,128)(2,1)}, bf16...) custom-call(s32[1]{0:T(128)} %bitcast.2.me_ref, ...), custom_call_target="tpu_custom_call" | custom-call | flops 4697620480 | bytes 13000000 | tf_op jit(solution)/shard_map/part_rows/pallas_call | solution.py:163
  94.4 1.8 collective-permute-start
  97.4 1.4 collective-permute-start.2
  98.9 1.5 collective-permute-start.3
  100.3 1.8 collective-permute-start.4
  102.2 1.5 collective-permute-start.5
  103.6 21.0 %collective-permute-done.1.refs_2_ = bf16[160,3584]{1,0:T(8,128)(2,1)S(1)} collective-permute-done((bf16[160,3584]{1,0:T(8,128)(2,1)}, bf16[160,3584]{1,0:T(8,128)(2,1)S(1)}, u32[]{:S(2)}, u32[]{:S(2)}) %collective-permute-start.1) | collective-permute-done | bytes 1146912 | tf_op jit(solution)/shard_map/ppermute | solution.py:524
  124.6 2.3 collective-permute-start.6
  126.9 22.8 %collective-permute-done.2.refs_3_ = bf16[160,3584]{1,0:T(8,128)(2,1)S(1)} collective-permute-done((bf16[160,3584]{1,0:T(8,128)(2,1)}, bf16[160,3584]{1,0:T(8,128)(2,1)S(1)}, u32[]{:S(2)}, u32[]{:S(2)}) %collective-permute-start.2) | collective-permute-done | bytes 1146912 | tf_op jit(solution)/shard_map/ppermute | solution.py:524
  149.6 25.0 %collective-permute-done.3.refs_4_ = bf16[160,3584]{1,0:T(8,128)(2,1)S(1)} collective-permute-done((bf16[160,3584]{1,0:T(8,128)(2,1)}, bf16[160,3584]{1,0:T(8,128)(2,1)S(1)}, u32[]{:S(2)}, u32[]{:S(2)}) %collective-permute-start.3) | collective-permute-done | bytes 1146912 | tf_op jit(solution)/shard_map/ppermute | solution.py:524
  174.7 24.6 %collective-permute-done.4.refs_5_ = bf16[160,3584]{1,0:T(8,128)(2,1)S(1)} collective-permute-done((bf16[160,3584]{1,0:T(8,128)(2,1)}, bf16[160,3584]{1,0:T(8,128)(2,1)S(1)}, u32[]{:S(2)}, u32[]{:S(2)}) %collective-permute-start.4) | collective-permute-done | bytes 1146912 | tf_op jit(solution)/shard_map/ppermute | solution.py:524
  199.3 1.5 collective-permute-done.6.refs_7_
  201.8 16.9 %pre.1.pre_ref = f32[1280,1024]{1,0:T(8,128)} custom-call(bf16[160,3584]{1,0:T(8,128)(2,1)} %get-tuple-element.12.refs_0_, bf16[160,3584]{1,0:T(8,128)(2,1)} %copy-done, bf16[160,3584]{1,0:T(8,128)(2,1)} %copy-done.1, bf16[160,3584]{1,0:T(8,128)(2,1)} %copy-done.2, bf16[160,3584]{1,0:T(8,128)(2,1)} %copy-done.3, bf16[160,3584]{1,0:T(8,128)(2,1)} %copy-done.4, ...), custom_call_target="tpu_custom_call" | custom-call | flops 9395240960 | bytes 22000000 | tf_op jit(solution)/shard_map/pre/pallas_call | solution.py:294
  218.7 34.5 %back_and_pieces.1 = bf16[1024,4608]{1,0:T(8,128)(2,1)} custom-call(s32[1]{0:T(128)} %bitcast.2.me_ref, bf16[1280,3584]{1,0:T(8,128)(2,1)} %bitcast.4.rows_ref, f32[1280,1024]{1,0:T(8,128)} %pre.1.pre_ref, bf16[1024,3584]{1,0:T(8,128)(2,1)} %bitcast.22, bf16[3584,1024]{1,0:T(8,128)(2,1)} %bitcast.21), custom_call_target="tpu_custom_call" | custom-call | flops 18790481920 | bytes 39000000 | tf_op jit(solution)/shard_map/back_and_pieces/pallas_call | solution.py:413
  253.2 119.3 %all_to_all.15 = bf16[128,8,4608]{2,1,0:T(8,128)(2,1)} all-to-all(bf16[128,8,4608]{2,1,0:T(8,128)(2,1)} %bitcast.16), channel_id=1, replica_groups=mesh['node'=16,'local'=8] {'node','local'}, dimensions={0} | all-to-all | bytes 18874368 | tf_op jit(solution)/shard_map/all_to_all | solution.py:517
  372.6 9.4 %combine.1 = (bf16[128,3584]{1,0:T(8,128)(2,1)}, f32[8,128]{1,0:T(8,128)}) custom-call(s32[8,128]{1,0:T(8,128)} %bitcast.18, s32[8,128]{1,0:T(8,128)} %bitcast.19, bf16[1024,4608]{1,0:T(8,128)(2,1)} %bitcast.13), custom_call_target="tpu_custom_call" | custom-call | tf_op jit(solution)/shard_map/combine/pallas_call | solution.py:492
  381.9 1.3 convert_bitcast_fusion
  (22 shorter events, 3.1 us)
Async XLA Ops:
  7.2 53.2 %all-gather.2.cloned.1.call-start = ((), (), s32[]{:S(2)}) async-start(), calls=%async_computation.3 | async-start | bytes 8552448 | tf_op jit(solution)/shard_map/all_gather | solution.py:536
  16.1 65.1 %all-to-all-start.1 = ((bf16[16,32,3712]{2,1,0:T(8,128)(2,1)}), bf16[16,32,3712]{2,1,0:T(8,128)(2,1)}, u32[]{:S(2)}, u32[]{:S(2)}) async-start(bf16[16,32,3712]{2,1,0:T(8,128)(2,1)} %bitcast.15), calls=%async_computation.1 | async-start | bytes 7602176 | tf_op jit(solution)/shard_map/all_to_all | solution.py:517
  81.2 137.5 %all-to-all-start = ((bf16[16,80,3584]{2,1,0:T(8,128)(2,1)}), bf16[16,80,3584]{2,1,0:T(8,128)(2,1)}, u32[]{:S(2)}, u32[]{:S(2)}) async-start(bf16[16,80,3584]{2,1,0:T(8,128)(2,1)} %bitcast.14), calls=%async_computation | async-start | bytes 18350080 | tf_op jit(solution)/shard_map/all_to_all | solution.py:517
  94.4 7.8 %collective-permute-start = (bf16[160,3584]{1,0:T(8,128)(2,1)}, bf16[160,3584]{1,0:T(8,128)(2,1)S(1)}, u32[]{:S(2)}, u32[]{:S(2)}) collective-permute-start(bf16[160,3584]{1,0:T(8,128)(2,1)} %get-tuple-element.13), channel_id=1, source_target_pairs={{0,1},{1,0},{2,3},{3,2},{4,5},{5,4},{6,7},{7,6},{8,9},{9,8},{10,11... | collective-permute-start | bytes 3440648 | tf_op jit(solution)/shard_map/ppermute | solution.py:524
  96.2 28.4 %collective-permute-start.1 = (bf16[160,3584]{1,0:T(8,128)(2,1)}, bf16[160,3584]{1,0:T(8,128)(2,1)S(1)}, u32[]{:S(2)}, u32[]{:S(2)}) collective-permute-start(bf16[160,3584]{1,0:T(8,128)(2,1)} %get-tuple-element.14), channel_id=1, source_target_pairs={{0,2},{1,3},{2,4},{3,5},{4,6},{5,7},{6,0},{7,1},{8,10},{9,11},{10,... | collective-permute-start | bytes 3440648 | tf_op jit(solution)/shard_map/ppermute | solution.py:524
  97.4 52.2 %collective-permute-start.2 = (bf16[160,3584]{1,0:T(8,128)(2,1)}, bf16[160,3584]{1,0:T(8,128)(2,1)S(1)}, u32[]{:S(2)}, u32[]{:S(2)}) collective-permute-start(bf16[160,3584]{1,0:T(8,128)(2,1)} %get-tuple-element.15), channel_id=1, source_target_pairs={{0,3},{1,2},{2,5},{3,4},{4,7},{5,6},{6,1},{7,0},{8,11},{9,10},{10,... | collective-permute-start | bytes 3440648 | tf_op jit(solution)/shard_map/ppermute | solution.py:524
  98.9 75.8 %collective-permute-start.3 = (bf16[160,3584]{1,0:T(8,128)(2,1)}, bf16[160,3584]{1,0:T(8,128)(2,1)S(1)}, u32[]{:S(2)}, u32[]{:S(2)}) collective-permute-start(bf16[160,3584]{1,0:T(8,128)(2,1)} %get-tuple-element.16), channel_id=1, source_target_pairs={{0,4},{1,5},{2,6},{3,7},{4,0},{5,1},{6,2},{7,3},{8,12},{9,13},{10,... | collective-permute-start | bytes 3440648 | tf_op jit(solution)/shard_map/ppermute | solution.py:524
  100.3 99.0 %collective-permute-start.4 = (bf16[160,3584]{1,0:T(8,128)(2,1)}, bf16[160,3584]{1,0:T(8,128)(2,1)S(1)}, u32[]{:S(2)}, u32[]{:S(2)}) collective-permute-start(bf16[160,3584]{1,0:T(8,128)(2,1)} %get-tuple-element.17), channel_id=1, source_target_pairs={{0,5},{1,4},{2,7},{3,6},{4,1},{5,0},{6,3},{7,2},{8,13},{9,12},{10,... | collective-permute-start | bytes 3440648 | tf_op jit(solution)/shard_map/ppermute | solution.py:524
  102.2 98.7 %copy-start = (bf16[160,3584]{1,0:T(8,128)(2,1)}, bf16[160,3584]{1,0:T(8,128)(2,1)S(1)}, u32[]{:S(2)}) copy-start(bf16[160,3584]{1,0:T(8,128)(2,1)S(1)} %collective-permute-done.refs_1_) | copy-start | bytes 3440644
  102.2 97.1 %collective-permute-start.5 = (bf16[160,3584]{1,0:T(8,128)(2,1)}, bf16[160,3584]{1,0:T(8,128)(2,1)S(1)}, u32[]{:S(2)}, u32[]{:S(2)}) collective-permute-start(bf16[160,3584]{1,0:T(8,128)(2,1)} %get-tuple-element.18), channel_id=1, source_target_pairs={{0,6},{1,7},{2,0},{3,1},{4,2},{5,3},{6,4},{7,5},{8,14},{9,15},{10,... | collective-permute-start | bytes 3440648 | tf_op jit(solution)/shard_map/ppermute | solution.py:524
  124.6 76.2 %copy-start.1 = (bf16[160,3584]{1,0:T(8,128)(2,1)}, bf16[160,3584]{1,0:T(8,128)(2,1)S(1)}, u32[]{:S(2)}) copy-start(bf16[160,3584]{1,0:T(8,128)(2,1)S(1)} %collective-permute-done.1.refs_2_) | copy-start | bytes 3440644
  124.6 76.2 %collective-permute-start.6 = (bf16[160,3584]{1,0:T(8,128)(2,1)}, bf16[160,3584]{1,0:T(8,128)(2,1)S(1)}, u32[]{:S(2)}, u32[]{:S(2)}) collective-permute-start(bf16[160,3584]{1,0:T(8,128)(2,1)} %get-tuple-element.19), channel_id=1, source_target_pairs={{0,7},{1,6},{2,1},{3,0},{4,3},{5,2},{6,5},{7,4},{8,15},{9,14},{10,... | collective-permute-start | bytes 3440648 | tf_op jit(solution)/shard_map/ppermute | solution.py:524
  149.6 51.2 %copy-start.2 = (bf16[160,3584]{1,0:T(8,128)(2,1)}, bf16[160,3584]{1,0:T(8,128)(2,1)S(1)}, u32[]{:S(2)}) copy-start(bf16[160,3584]{1,0:T(8,128)(2,1)S(1)} %collective-permute-done.2.refs_3_) | copy-start | bytes 3440644
  174.7 26.2 %copy-start.3 = (bf16[160,3584]{1,0:T(8,128)(2,1)}, bf16[160,3584]{1,0:T(8,128)(2,1)S(1)}, u32[]{:S(2)}) copy-start(bf16[160,3584]{1,0:T(8,128)(2,1)S(1)} %collective-permute-done.3.refs_4_) | copy-start | bytes 3440644
  199.3 1.5 copy-start.4
  199.3 1.5 copy-start.5
  200.8 1.0 copy-start.6
Sparse Core Ops, SparseCore 0:
  10.4 49.9 all-gather.1

commit v3 on v2

--- a/solution.py
+++ b/solution.py
@@ -35,29 +35,6 @@
     return lax.dot_general(a, b, (((0,), (0,)), ((), ())), preferred_element_type=F32)
 
 
-def slots_of(ids, first):
-    tok = ids.shape[1]
-    expert = first + iota((GROUP, tok), 0)
-    hit = jnp.zeros((GROUP, tok), F32)
-    for slot in range(ids.shape[0]):
-        hit = hit + (expert == ids[slot : slot + 1, :]).astype(F32)
-    earlier = (iota((tok, tok), 0) < iota((tok, tok), 1)).astype(BF16)
-    before = dot(hit.astype(BF16), earlier)
-    place = jnp.where(hit > 0.5, before, -1.0)
-    rows = GROUP * MAIN
-    spread = (iota((rows, GROUP), 0) // MAIN == iota((rows, GROUP), 1)).astype(BF16)
-    return dot(spread, place.astype(BF16)), spread, expert
-
-
-def picks(ids, first):
-    place, spread, expert = slots_of(ids, first)
-    row = iota(place.shape, 0)
-    main = place == (row % MAIN).astype(F32)
-    tail = place == (MAIN + row % 2).astype(F32)
-    quarter = (row % MAIN) // 2
-    return main, tail, quarter, spread, expert
-
-
 def places(ids, first, count):
     tok = ids.shape[1]
     expert = first + iota((count, tok), 0)
@@ -68,7 +45,7 @@
     return jnp.where(hit > 0.5, dot(hit.astype(BF16), earlier), -1.0), expert
 
 
-def node_kernel(ids_ref, x_ref, out_ref, *, share, nodes, local):
+def node_kernel(ids_ref, x_ref, dy_ref, out_ref, marked_ref, *, share, nodes, local):
     width = x_ref.shape[1]
     tok = x_ref.shape[0]
     rows = out_ref.shape[0]
@@ -91,28 +68,42 @@
     slots = jnp.where(iota((rows, count), 0) // share == iota((rows, count), 1) // local, slots, 0.0)
     lanes = (iota((count, EXTRA), 0) % local == iota((count, EXTRA), 1)).astype(BF16)
     out_ref[:, width:] = dot(slots.astype(BF16), lanes).astype(BF16)
-
-
-def node_rows(ids_t, x, nodes, local):
+    own = iota((ids.shape[0], EXTRA), 0) == iota((ids.shape[0], EXTRA), 1)
+    marked_ref[:, :width] = dy_ref[...]
+    part = marked_ref.shape[0]
+    here = (iota((part, tok), 0) + pl.program_id(0) * part == iota((part, tok), 1)).astype(BF16)
+    by_token = dot_tn(ids.astype(F32).astype(BF16), own.astype(BF16)).astype(BF16)
+    marked_ref[:, width:] = dot(here, by_token).astype(BF16)
+
+
+def node_rows(ids_t, x, dy, nodes, local):
     top, tok = ids_t.shape
     width = x.shape[1]
     share = tok * NODES_MAX // nodes
     steps = 4
+    part = tok // steps
     return pl.pallas_call(
         functools.partial(node_kernel, share=share, nodes=nodes, local=local),
         grid=(steps,),
         in_specs=[
             pl.BlockSpec((top, tok), lambda i: (0, 0)),
             pl.BlockSpec((tok, width), lambda i: (0, 0)),
-        ],
-        out_specs=pl.BlockSpec((nodes * share // steps, width + EXTRA), lambda i: (i, 0)),
-        out_shape=jax.ShapeDtypeStruct((nodes * share, width + EXTRA), BF16),
+            pl.BlockSpec((part, width), lambda i: (i, 0)),
+        ],
+        out_specs=[
+            pl.BlockSpec((nodes * share // steps, width + EXTRA), lambda i: (i, 0)),
+            pl.BlockSpec((part, width + EXTRA), lambda i: (i, 0)),
+        ],
+        out_shape=[
+            jax.ShapeDtypeStruct((nodes * share, width + EXTRA), BF16),
+            jax.ShapeDtypeStruct((tok, width + EXTRA), BF16),
+        ],
         compiler_params=pltpu.CompilerParams(vmem_limit_bytes=VMEM),
         cost_estimate=pl.CostEstimate(
-            flops=2 * nodes * share * 256 * width, bytes_accessed=5_000_000, transcendentals=0
+            flops=2 * nodes * share * 256 * width, bytes_accessed=7_000_000, transcendentals=0
         ),
         name="node_rows",
-    )(ids_t, x)
+    )(ids_t, x, dy)
 
 
 def part_kernel(me_ref, rows_ref, slots_ref, *refs, share, nodes, local):
@@ -182,23 +173,18 @@
     )(me, rows, rows)
 
 
-def gathered_kernel(me_ref, rows_ref, ids_ref, out_ref, main_ref, tail_ref, *, tok, nodes, local):
-    x, c = me_ref[0] // 2, me_ref[0] % 2
-    chips = local // 2
-    both = 2 * tok
+def gathered_kernel(me_ref, *refs, tok, nodes, local):
+    rows_refs, ids_refs, (out_ref, main_ref, tail_ref) = refs[:local], refs[local : 2 * local], refs[2 * local :]
     pair = 2 * MAIN
     per_node = local * CAP
-
-    def chip_at(d):
-        return (x + chips - d) % chips
 
     @pl.when(pl.program_id(0) == 0)
     def _():
         lane = iota((tok, EXTRA), 1)
         earlier = (iota((tok, tok), 1) < iota((tok, tok), 0)).astype(BF16)
 
-        def place_of(source):
-            ids = ids_ref[pl.ds(source * tok, tok), :].astype(F32)
+        def place_of(ids_ref):
+            ids = ids_ref[...].astype(F32)
             hit = jnp.zeros((tok, EXTRA), F32)
             for slot in range(TOP):
                 hit = hit + (ids[:, slot : slot + 1] == (lane * local + me_ref[0]).astype(F32)).astype(F32)
@@ -206,24 +192,23 @@
 
         shape = (nodes * pair, EXTRA)
         spread = (iota(shape, 0) // pair == iota(shape, 1)).astype(BF16)
-        shape = (nodes * pair, both)
+        shape = (nodes * pair, 2 * tok)
         row, at = iota(shape, 0), iota(shape, 1)
         core = at // tok
-        main_fits = core == ((row % pair) // MAIN + c) % 2
+        main_fits = core == (row % pair) // MAIN
         main_slot = (row % MAIN).astype(F32)
-        tail_fits = core == ((row % pair) // 2 % 2 + c) % 2
+        tail_fits = core == (row % pair) // 2 % 2
         tail_slot = (MAIN + row % 2).astype(F32)
-        for d in range(chips):
-            a = chip_at(d)
-            place = jnp.concatenate([place_of(2 * a), place_of(2 * a + 1)], axis=0)
+        for d in range(local // 2):
+            place = jnp.concatenate([place_of(ids_refs[2 * d]), place_of(ids_refs[2 * d + 1])], axis=0)
             place = dot_nt(spread, place)
             main_ref[d] = jnp.logical_and(place == main_slot, main_fits).astype(BF16)
             here = jnp.logical_and(tail_fits, (row % pair) // 4 == d)
             tail_ref[d] = jnp.logical_and(place == tail_slot, here).astype(BF16)
 
     tail = None
-    for d in range(chips):
-        rows = rows_ref[pl.ds(pl.multiple_of(chip_at(d) * both, both), both), :]
+    for d in range(local // 2):
+        rows = jnp.concatenate([rows_refs[2 * d][...], rows_refs[2 * d + 1][...]], axis=0)
         got = dot(main_ref[d], rows).astype(BF16)
         for n in range(nodes):
             out_ref[n * per_node + d * pair : n * per_node + (d + 1) * pair, :] = got[n * pair : (n + 1) * pair, :]
@@ -234,45 +219,40 @@
         out_ref[n * per_node + local * MAIN : (n + 1) * per_node, :] = tail[n * pair : (n + 1) * pair, :]
 
 
-def gathered_rows(me, rows, nodes, local):
-    total, wide = rows.shape
+def gathered_rows(me, parts, nodes, local):
+    tok, wide = parts[0].shape
     width = wide - EXTRA
-    tok = total // local
-    fold = width // QUARTERS
+    tile = width // 7
     size = nodes * local * CAP
-    pair = 2 * MAIN
+    picks = pltpu.VMEM((local // 2, nodes * 2 * MAIN, 2 * tok), BF16)
     return pl.pallas_call(
         functools.partial(gathered_kernel, tok=tok, nodes=nodes, local=local),
-        grid=(QUARTERS,),
-        in_specs=[
-            pl.BlockSpec(memory_space=pltpu.SMEM),
-            pl.BlockSpec((total, fold), lambda i: (0, i)),
-            pl.BlockSpec((total, EXTRA), lambda i: (0, width // EXTRA)),
-        ],
-        out_specs=pl.BlockSpec((size, fold), lambda i: (0, i)),
+        grid=(width // tile,),
+        in_specs=[pl.BlockSpec(memory_space=pltpu.SMEM)]
+        + [pl.BlockSpec((tok, tile), lambda i: (0, i))] * local
+        + [pl.BlockSpec((tok, EXTRA), lambda i: (0, width // EXTRA))] * local,
+        out_specs=pl.BlockSpec((size, tile), lambda i: (0, i)),
         out_shape=jax.ShapeDtypeStruct((size, width), BF16),
-        scratch_shapes=[
-            pltpu.VMEM((local // 2, nodes * pair, 2 * tok), BF16),
-            pltpu.VMEM((local // 2, nodes * pair, 2 * tok), BF16),
-        ],
+        scratch_shapes=[picks, picks],
         compiler_params=pltpu.CompilerParams(vmem_limit_bytes=VMEM),
         cost_estimate=pl.CostEstimate(
             flops=4 * size * 256 * width, bytes_accessed=17_000_000, transcendentals=0
         ),
         name="gathered_rows",
-    )(me, rows, rows)
-
-
-def pre_kernel(*refs, nodes, local):
-    rows_refs, (w_ref, out_ref, rows_ref, made_ref, sems) = refs[:local], refs[local:]
+    )(me, *parts, *parts)
+
+
+def pre_kernel(*refs, nodes):
+    rows_refs, (w_ref, out_ref, rows_ref, made_ref, sems) = refs[:-5], refs[-5:]
+    count = len(rows_refs)
     size = nodes * CAP
-    per_node = local * CAP
+    per_node = count * CAP
 
     @pl.when(pl.program_id(0) == 0)
     def _():
         copies = [
-            pltpu.make_async_copy(rows_refs[rel], rows_ref.at[pl.ds(rel * size, size), :], sems.at[rel])
-            for rel in range(local)
+            pltpu.make_async_copy(rows_refs[i], rows_ref.at[pl.ds(i * size, size), :], sems.at[i])
+            for i in range(count)
         ]
         for copy in copies:
             copy.start()
@@ -281,37 +261,38 @@
 
     made_ref[...] = dot(rows_ref[...], w_ref[...])
     for n in range(nodes):
-        for rel in range(local):
-            to, at = n * per_node + rel * MAIN, rel * size + n * MAIN
+        for i in range(count):
+            to, at = n * per_node + i * MAIN, i * size + n * MAIN
             out_ref[to : to + MAIN, :] = made_ref[at : at + MAIN, :]
-            to, at = n * per_node + local * MAIN + rel * 2, rel * size + nodes * MAIN + n * 2
+            to, at = n * per_node + count * MAIN + i * 2, i * size + nodes * MAIN + n * 2
             out_ref[to : to + 2, :] = made_ref[at : at + 2, :]
 
 
-def pre_of(parts, w_up, nodes, local, tile=256):
+def pre_of(parts, w_up, nodes, tile=256):
     width, hid = w_up.shape
-    total = nodes * local * CAP
+    count = len(parts)
+    total = nodes * count * CAP
     return pl.pallas_call(
-        functools.partial(pre_kernel, nodes=nodes, local=local),
+        functools.partial(pre_kernel, nodes=nodes),
         grid=(hid // tile,),
-        in_specs=[pl.BlockSpec(memory_space=pl.ANY)] * local + [pl.BlockSpec((width, tile), lambda i: (0, i))],
+        in_specs=[pl.BlockSpec(memory_space=pl.ANY)] * count + [pl.BlockSpec((width, tile), lambda i: (0, i))],
         out_specs=pl.BlockSpec((total, tile), lambda i: (0, i)),
         out_shape=jax.ShapeDtypeStruct((total, hid), F32),
         scratch_shapes=[
             pltpu.VMEM((total, width), BF16),
             pltpu.VMEM((total, tile), F32),
-            pltpu.SemaphoreType.DMA((local,)),
+            pltpu.SemaphoreType.DMA((count,)),
         ],
         compiler_params=pltpu.CompilerParams(vmem_limit_bytes=VMEM),
         cost_estimate=pl.CostEstimate(
-            flops=2 * total * width * hid, bytes_accessed=22_000_000, transcendentals=0
+            flops=2 * total * width * hid, bytes_accessed=15_000_000, transcendentals=0
         ),
         name="pre",
     )(*parts, w_up)
 
 
 def back_kernel(
-    me_ref, rows_ref, pre_ref, down_ref, up_ref, out_ref, raw_ref, inner_ref, gate_ref, piece_ref, stack_ref, fold_ref, extra_ref, sems, *, local
+    me_ref, rows_ref, early_ref, late_ref, down_ref, up_ref, out_ref, raw_ref, inner_ref, gate_ref, piece_ref, stack_ref, fold_ref, extra_ref, sems, pre_ref, *, local
 ):
     step = pl.program_id(0)
     width = down_ref.shape[1]
@@ -328,6 +309,14 @@
 
         @pl.when(step == j)
         def _():
+            mains, lasts = local // 2 * MAIN, local // 2 * 2
+            half = mains + lasts
+            for n in range(main // (local * MAIN)):
+                for h, ref in enumerate((early_ref, late_ref)):
+                    to = n * 2 * half + h * mains
+                    pre_ref[to : to + mains, :] = ref[n * half : n * half + mains, :]
+                    to = n * 2 * half + 2 * mains + h * lasts
+                    pre_ref[to : to + lasts, :] = ref[n * half + mains : (n + 1) * half, :]
             pre = pre_ref[...]
             back = dot_nt(rows_ref[...], down_ref[...])
             sig = 1.0 / (1.0 + jnp.exp(-pre))
@@ -404,7 +393,7 @@
                 fold_copy.wait()
 
 
-def pieces_of(me, rows, pre, w_down, w_up, local, tile=256):
+def pieces_of(me, rows, early, late, w_down, w_up, local, tile=256):
     total, width = rows.shape
     hid = w_down.shape[0]
     main = total // CAP * MAIN
@@ -416,7 +405,8 @@
         in_specs=[
             pl.BlockSpec(memory_space=pltpu.SMEM),
             pl.BlockSpec((total, width), lambda i: (0, 0), pipeline_mode=pl.Buffered(1)),
-            pl.BlockSpec((total, tile), lambda i: (0, jnp.minimum(i, first - 1))),
+            pl.BlockSpec((total // 2, tile), lambda i: (0, jnp.minimum(i, first - 1))),
+            pl.BlockSpec((total // 2, tile), lambda i: (0, jnp.minimum(i, first - 1))),
             pl.BlockSpec((tile, width), lambda i: (jnp.minimum(i, first - 1), 0)),
             pl.BlockSpec((fold, hid), lambda i: (jnp.maximum(i - first, 0), 0)),
         ],
@@ -431,84 +421,104 @@
             pltpu.VMEM((main, fold), BF16),
             pltpu.VMEM((main, EXTRA), BF16),
             pltpu.SemaphoreType.DMA((4,)),
+            pltpu.VMEM((total, tile), F32),
         ],
         compiler_params=pltpu.CompilerParams(vmem_limit_bytes=VMEM),
         cost_estimate=pl.CostEstimate(
             flops=4 * total * width * hid, bytes_accessed=39_000_000, transcendentals=total * hid
         ),
         name="back_and_pieces",
-    )(me, rows, pre, w_down, w_up)
-
-
-def combine_kernel(ids_ref, gate_ref, rows_ref, out_ref, grad_ref, acc_ref, sum_ref):
+    )(me, rows, early, late, w_down, w_up)
+
+
+def combine_kernel(ids_ref, gate_ref, rows_ref, fold_ref, extra_ref, out_ref, grad_ref, main_ref, last_ref, tail_ref):
     step = pl.program_id(0)
-    tok, width = out_ref.shape
-    fold = width // QUARTERS
-    ids = ids_ref[...]
-    main, tail, quarter, spread, expert = picks(ids, step * GROUP)
-    high = jnp.zeros(expert.shape, F32)
-    low = jnp.zeros(expert.shape, F32)
-    for slot in range(ids.shape[0]):
-        same = expert == ids[slot : slot + 1, :]
-        fixed = gate_ref[slot : slot + 1, :]
-        high = high + jnp.where(same, (fixed // 256).astype(F32), 0.0)
-        low = low + jnp.where(same, (fixed % 256).astype(F32), 0.0)
-    high = dot(spread, high.astype(BF16)) * (1.0 / 256.0)
-    low = dot(spread, low.astype(BF16)) * (1.0 / 65536.0)
-
-    def weights(mask):
-        return jnp.concatenate([jnp.where(mask, high, 0.0), jnp.where(mask, low, 0.0)], axis=1).astype(BF16)
+    top, tok = ids_ref.shape
+    fold = fold_ref.shape[1]
+    size = GROUP * MAIN
+    tails = 2 * GROUP
+    groups = rows_ref.shape[0] // size
 
     @pl.when(step == 0)
     def _():
-        acc_ref[...] = jnp.zeros_like(acc_ref)
-        sum_ref[...] = jnp.zeros_like(sum_ref)
-
-    both = dot_tn(weights(main), rows_ref[:, :width])
-    acc_ref[...] += both[:tok, :] + both[tok:, :]
-    for q in range(QUARTERS):
-        both = dot_tn(weights(jnp.logical_and(tail, quarter == q)), rows_ref[:, width : width + fold])
-        acc_ref[:, q * fold : (q + 1) * fold] += both[:tok, :] + both[tok:, :]
-
-    extra = rows_ref[:, width + fold :].astype(F32)
-    value = jnp.where(main, extra[:, 0:1], 0.0) + jnp.where(
-        jnp.logical_and(tail, quarter == 0), extra[:, EXTRA // 2 : EXTRA // 2 + 1], 0.0
-    )
-    value = dot_tn(spread, value.astype(BF16))
-    for slot in range(ids.shape[0]):
-        part = jnp.sum(jnp.where(expert == ids[slot : slot + 1, :], value, 0.0), axis=0, keepdims=True)
-        sum_ref[slot : slot + 1, :] = sum_ref[slot : slot + 1, :] + part
-
-    @pl.when(step == pl.num_programs(0) - 1)
-    def _():
-        out_ref[...] = acc_ref[...].astype(BF16)
-        grad_ref[...] = sum_ref[...]
+        ids = ids_ref[...]
+        to = iota((size, size), 0)
+        unfold = ((to % tails) // 2) * MAIN + (to // tails) * 2 + to % 2
+        unfold = (unfold == iota((size, size), 1)).astype(BF16)
+        spread = (iota((size, GROUP), 0) // MAIN == iota((size, GROUP), 1)).astype(BF16)
+        twice = (iota((tails, GROUP), 0) // 2 == iota((tails, GROUP), 1)).astype(BF16)
+        row, last_row = iota((size, tok), 0), iota((tails, tok), 0)
+        grads = [jnp.zeros((1, tok), F32) for _ in range(top)]
+        for b in range(groups):
+            place, expert = places(ids, b * GROUP, GROUP)
+            place = place.astype(BF16)
+            high = jnp.zeros(expert.shape, F32)
+            low = jnp.zeros(expert.shape, F32)
+            for slot in range(top):
+                same = expert == ids[slot : slot + 1, :]
+                fixed = gate_ref[slot : slot + 1, :]
+                high = high + jnp.where(same, (fixed // 256).astype(F32), 0.0)
+                low = low + jnp.where(same, (fixed % 256).astype(F32), 0.0)
+            gates = jnp.concatenate([high, low], axis=1).astype(BF16)
+
+            def weights(copies, slots):
+                mask = dot(copies, place) == slots.astype(F32)
+                both = dot(copies, gates)
+                scaled = [both[:, :tok] * (1.0 / 256.0), both[:, tok:] * (1.0 / 65536.0)]
+                return mask, jnp.concatenate([jnp.where(mask, part, 0.0) for part in scaled], axis=1)
+
+            main, weight = weights(spread, row % MAIN)
+            main_ref[:, b * size : (b + 1) * size] = weight.T.astype(BF16)
+            tail, weight = weights(twice, MAIN + last_row % 2)
+            last_ref[:, b * tails : (b + 1) * tails] = weight.T.astype(BF16)
+            stack = dot(unfold, fold_ref[b * size : (b + 1) * size, :]).astype(BF16)
+            for q in range(QUARTERS):
+                tail_ref[q, b * tails : (b + 1) * tails, :] = stack[q * tails : (q + 1) * tails, :]
+            extra = extra_ref[b * size : (b + 1) * size, :]
+            value = jnp.where(main, extra[:, 0:1].astype(F32), 0.0)
+            last = dot(unfold[:tails, :], extra)[:, EXTRA // 2 : EXTRA // 2 + 1]
+            last = jnp.where(tail, last, 0.0)
+            value = dot_tn(spread, value.astype(BF16)) + dot_tn(twice, last.astype(BF16))
+            for slot in range(top):
+                same = expert == ids[slot : slot + 1, :]
+                grads[slot] = grads[slot] + jnp.sum(jnp.where(same, value, 0.0), axis=0, keepdims=True)
+        grad_ref[...] = jnp.concatenate(grads, axis=0).astype(BF16)
+
+    both = dot(main_ref[...], rows_ref[...]) + dot(last_ref[...], tail_ref[step])
+    out_ref[...] = (both[:tok, :] + both[tok:, :]).astype(BF16)
 
 
 def combine(ids_t, gate_t, rows, width):
     top, tok = ids_t.shape
     main, wide = rows.shape
-    size = GROUP * MAIN
+    fold = width // QUARTERS
+    tails = main // QUARTERS
     return pl.pallas_call(
         combine_kernel,
-        grid=(main // size,),
+        grid=(QUARTERS,),
         in_specs=[
             pl.BlockSpec((top, tok), lambda i: (0, 0)),
             pl.BlockSpec((top, tok), lambda i: (0, 0)),
-            pl.BlockSpec((size, wide), lambda i: (i, 0)),
+            pl.BlockSpec((main, fold), lambda i: (0, i)),
+            pl.BlockSpec((main, fold), lambda i: (0, QUARTERS)),
+            pl.BlockSpec((main, EXTRA), lambda i: (0, (width + fold) // EXTRA)),
         ],
         out_specs=[
-            pl.BlockSpec((tok, width), lambda i: (0, 0)),
+            pl.BlockSpec((tok, fold), lambda i: (0, i)),
             pl.BlockSpec((top, tok), lambda i: (0, 0)),
         ],
         out_shape=[
             jax.ShapeDtypeStruct((tok, width), BF16),
-            jax.ShapeDtypeStruct((top, tok), F32),
-        ],
-        scratch_shapes=[pltpu.VMEM((tok, width), F32), pltpu.VMEM((top, tok), F32)],
+            jax.ShapeDtypeStruct((top, tok), BF16),
+        ],
+        scratch_shapes=[
+            pltpu.VMEM((2 * tok, main), BF16),
+            pltpu.VMEM((2 * tok, tails), BF16),
+            pltpu.VMEM((QUARTERS, tails, fold), BF16),
+        ],
         compiler_params=pltpu.CompilerParams(vmem_limit_bytes=VMEM),
         name="combine",
-    )(ids_t, gate_t, rows)
+    )(ids_t, gate_t, rows, rows, rows)
 
 
 def exchange(rows, axes):
@@ -530,18 +540,18 @@
     ids_t = expert_ids.T
     gate_t = gate_fixed.T
     me = lax.axis_index("local").astype(jnp.int32).reshape(1)
-    marked = jnp.concatenate(
-        [cotangent, jnp.pad(expert_ids.astype(BF16), ((0, 0), (0, EXTRA - expert_ids.shape[1])))], axis=1
-    )
-    rows_dy = lax.all_gather(marked, "local", tiled=True)
-    rows_x = exchange(node_rows(ids_t, tokens, nodes, local), "node")
-    rows_dy = exchange(gathered_rows(me, rows_dy, nodes, local), "node")
+    send_x, marked = node_rows(ids_t, tokens, cotangent, nodes, local)
+    rows_x = exchange(send_x, "node")
+    same = [marked] + [shift(marked, 2 * d, local) for d in range(1, local // 2)]
+    all_dy = [part for rows in same for part in (rows, shift(rows, 1, local))]
+    rows_dy = exchange(gathered_rows(me, all_dy, nodes, local), "node")
     parts = part_rows(me, rows_x, nodes, local)
     parts = [parts[0]] + [shift(parts[rel], rel, local) for rel in range(1, local)]
-    pre = pre_of(parts, w_up[0], nodes, local)
-    pieces = pieces_of(me, rows_dy, pre, w_down[0], w_up[0], local)
+    early = pre_of(parts[: local // 2], w_up[0], nodes)
+    late = pre_of(parts[local // 2 :], w_up[0], nodes)
+    pieces = pieces_of(me, rows_dy, early, late, w_down[0], w_up[0], local)
     grad_input, grad_gate = combine(ids_t, gate_t, exchange(pieces, ("node", "local")), width)
-    return grad_input, grad_gate.T.astype(BF16)
+    return grad_input, grad_gate.T
 
 
 def solution(mesh):

time: 391 us -> 383 us (0.980)
  starting transfers between devices: 25 us -> 52.2 us
  waiting for transfers between devices: 141 us -> 117 us
  between operations: 14.1 us -> 0.72 us
  Pallas kernels: 85.8 us -> 92.4 us
  other arithmetic: 4.14 us -> 0 us
    all_gather x1 -> x0, waiting for transfers between devices: 35.6 us -> none  [per_device(): rows_dy = lax.all_gather(marked, 'local', tiled=True)]
    ppermute x7 -> x14, starting transfers between devices: 11.5 us -> 36.7 us  [shift(): return lax.ppermute(rows, 'local', pairs)]
    ppermute x7 -> x14, waiting for transfers between devices: 94.9 us -> 106 us  [shift(): return lax.ppermute(rows, 'local', pairs)]
    pallas_call x2 -> x3, Pallas kernels: 26.2 us -> 31 us  [the longest x2 21.6 us: pre_of(): pl.pallas_call(functools.partial(pre_kernel, nodes=nodes), grid=(hid // t...]
  transfers between devices with their start and end apart: 10 -> 16, of which waited for: 7 -> 9; matrix products, arithmetic and copies ran while one was open for 0% -> 0% of each run, Pallas kernels for 11% -> 11%
where the time goes in v3:
time: 383 us; the launch traced here: 382 us
  waiting for transfers between devices  117 us (31%)
  blocking collectives  117 us (31%)
  Pallas kernels  92.4 us (24%)
  starting transfers between devices  52.2 us (14%)
    all_to_all x1, blocking collectives, exchange(): lax.all_to_all(blocks, axes, split_axis=0, concat_axis=0, tiled=True)  117 us
    ppermute x14, waiting for transfers between devices, shift(): return lax.ppermute(rows, 'local', pairs)  106 us
    ppermute x14, starting transfers between devices, shift(): return lax.ppermute(rows, 'local', pairs)  36.7 us
    pallas_call x1, Pallas kernels, pieces_of(): pl.pallas_call(functools.partial(back_kernel, local=local), grid=(first +...  34.2 us
    pallas_call x2, Pallas kernels, pre_of(): pl.pallas_call(functools.partial(pre_kernel, nodes=nodes), grid=(hid // t...  21.6 us
    all_to_all x2, starting transfers between devices, exchange(): lax.all_to_all(blocks, axes, split_axis=0, concat_axis=0, tiled=True)  15.4 us
    pallas_call x1, Pallas kernels, gathered_rows(): pl.pallas_call(functools.partial(gathered_kernel, tok=tok, nodes=nodes, l...  12.5 us
    all_to_all x2, waiting for transfers between devices, exchange(): lax.all_to_all(blocks, axes, split_axis=0, concat_axis=0, tiled=True)  11 us
  transfers between devices with their start and end apart: 16, of which 9 were waited for; matrix products, arithmetic and copies ran while one was open for 0% of the time, Pallas kernels for 11%

profile of v3, /device:TPU:1, one launch (start us, length us, event | category | flops | bytes accessed | tf_op | source)
XLA Modules:
  0.0 382.2 jit_solution(178419875356842764)
XLA Ops:
  0.6 6.5 %node_rows.1 = (bf16[512,3712]{1,0:T(8,128)(2,1)}, bf16[128,3712]{1,0:T(8,128)(2,1)}) custom-call(s32[8,128]{1,0:T(8,128)} %bitcast.18, bf16[128,3584]{1,0:T(8,128)(2,1)} %x_ref.1, bf16[128,3584]{1,0:T(8,128)(2,1)} %dy_ref.1), custom_call_target="tpu_custom_call" | custom-call | flops 939524096 | bytes 7000000 | tf_op jit(solution)/shard_map/node_rows/pallas_call | solution.py:85
  7.1 8.8 %all-to-all-start.1 = ((bf16[16,32,3712]{2,1,0:T(8,128)(2,1)}), bf16[16,32,3712]{2,1,0:T(8,128)(2,1)}, u32[]{:S(2)}, u32[]{:S(2)}) async-start(bf16[16,32,3712]{2,1,0:T(8,128)(2,1)} %bitcast.17), calls=%async_computation.1 | async-start | bytes 7602176 | tf_op jit(solution)/shard_map/all_to_all | solution.py:527
  15.9 2.5 collective-permute-start.5
  19.6 1.8 collective-permute-start
  21.4 17.2 %collective-permute-done.5.refs_6_.refs_14_ = bf16[128,3712]{1,0:T(8,128)(2,1)S(1)} collective-permute-done((bf16[128,3712]{1,0:T(8,128)(2,1)S(1)}, bf16[128,3712]{1,0:T(8,128)(2,1)S(1)}, u32[]{:S(2)}, u32[]{:S(2)}) %collective-permute-start.5) | collective-permute-done | bytes 950304 | tf_op jit(solution)/shard_map/ppermute | solution.py:534
  38.6 21.5 %collective-permute-start.6 = (bf16[128,3712]{1,0:T(8,128)(2,1)S(1)}, bf16[128,3712]{1,0:T(8,128)(2,1)}, u32[]{:S(2)}, u32[]{:S(2)}) collective-permute-start(bf16[128,3712]{1,0:T(8,128)(2,1)S(1)} %collective-permute-done.5.refs_6_.refs_14_), channel_id=1, source_target_pairs={{0,1},{1,0},{2,3},{3,2},{4,5},{5,4},{6,7},{7,6},{8,9},{9,8},{10,11... | collective-permute-start | bytes 2850824 | tf_op jit(solution)/shard_map/ppermute | solution.py:534
  60.2 3.2 collective-permute-done.1.refs_2_.refs_10_
  63.9 2.5 collective-permute-done.2.refs_3_.refs_11_
  66.4 12.5 %gathered_rows.1 = bf16[1280,3584]{1,0:T(8,128)(2,1)} custom-call(s32[1]{0:T(128)} %bitcast.2.me_ref, bf16[128,3712]{1,0:T(8,128)(2,1)} %get-tuple-element.14.refs_0_.refs_8_, bf16[128,3712]{1,0:T(8,128)(2,1)} %collective-permute-done.refs_1_.refs_9_, bf16[128,3712]{1,0:T(8,128)(2,1)} %collective-permute-done.1.refs_2_.refs_10_, ...), custom_call_target="tpu_custom_call" | custom-call | flops 4697620480 | bytes 17000000 | tf_op jit(solution)/shard_map/gathered_rows/pallas_call | solution.py:228
  78.9 6.7 %all-to-all-start = ((bf16[16,80,3584]{2,1,0:T(8,128)(2,1)}), bf16[16,80,3584]{2,1,0:T(8,128)(2,1)}, u32[]{:S(2)}, u32[]{:S(2)}) async-start(bf16[16,80,3584]{2,1,0:T(8,128)(2,1)} %bitcast.15), calls=%async_computation | async-start | bytes 18350080 | tf_op jit(solution)/shard_map/all_to_all | solution.py:527
  85.5 8.3 %part_rows.1 = (bf16[160,3584]{1,0:T(8,128)(2,1)}, bf16[160,3584]{1,0:T(8,128)(2,1)}, bf16[160,3584]{1,0:T(8,128)(2,1)}, bf16[160,3584]{1,0:T(8,128)(2,1)}, bf16...) custom-call(s32[1]{0:T(128)} %bitcast.2.me_ref, ...), custom_call_target="tpu_custom_call" | custom-call | flops 4697620480 | bytes 13000000 | tf_op jit(solution)/shard_map/part_rows/pallas_call | solution.py:154
  95.0 3.7 collective-permute-start.10
  98.7 2.1 collective-permute-start.12
  100.8 22.1 %collective-permute-done.8.refs_2_ = bf16[160,3584]{1,0:T(8,128)(2,1)S(1)} collective-permute-done((bf16[160,3584]{1,0:T(8,128)(2,1)}, bf16[160,3584]{1,0:T(8,128)(2,1)S(1)}, u32[]{:S(2)}, u32[]{:S(2)}) %collective-permute-start.8) | collective-permute-done | bytes 1146912 | tf_op jit(solution)/shard_map/ppermute | solution.py:534
  122.9 2.2 collective-permute-start.13
  125.1 22.8 %collective-permute-done.9.refs_3_ = bf16[160,3584]{1,0:T(8,128)(2,1)S(1)} collective-permute-done((bf16[160,3584]{1,0:T(8,128)(2,1)}, bf16[160,3584]{1,0:T(8,128)(2,1)S(1)}, u32[]{:S(2)}, u32[]{:S(2)}) %collective-permute-start.9) | collective-permute-done | bytes 1146912 | tf_op jit(solution)/shard_map/ppermute | solution.py:534
  149.0 10.8 %pre.2.early_ref = f32[640,1024]{1,0:T(8,128)} custom-call(bf16[160,3584]{1,0:T(8,128)(2,1)} %get-tuple-element.16.refs_0_, bf16[160,3584]{1,0:T(8,128)(2,1)} %copy-done.5, bf16[160,3584]{1,0:T(8,128)(2,1)} %copy-done.7, bf16[160,3584]{1,0:T(8,128)(2,1)} %copy-done.8, bf16[3584,1024]{1,0:T(8,128)(2,1)} %bitcast.21), custom_call_target="tpu_custom_call" | custom-call | flops 4697620480 | bytes 15000000 | tf_op jit(solution)/shard_map/pre/pallas_call | solution.py:275
  159.8 13.1 %collective-permute-done.10.refs_0_ = bf16[160,3584]{1,0:T(8,128)(2,1)S(1)} collective-permute-done((bf16[160,3584]{1,0:T(8,128)(2,1)}, bf16[160,3584]{1,0:T(8,128)(2,1)S(1)}, u32[]{:S(2)}, u32[]{:S(2)}) %collective-permute-start.10) | collective-permute-done | bytes 1146912 | tf_op jit(solution)/shard_map/ppermute | solution.py:534
  172.9 24.6 %collective-permute-done.11.refs_1_ = bf16[160,3584]{1,0:T(8,128)(2,1)S(1)} collective-permute-done((bf16[160,3584]{1,0:T(8,128)(2,1)}, bf16[160,3584]{1,0:T(8,128)(2,1)S(1)}, u32[]{:S(2)}, u32[]{:S(2)}) %collective-permute-start.11) | collective-permute-done | bytes 1146912 | tf_op jit(solution)/shard_map/ppermute | solution.py:534
  200.0 10.8 %pre.3.late_ref = f32[640,1024]{1,0:T(8,128)} custom-call(bf16[160,3584]{1,0:T(8,128)(2,1)} %copy-done.3, bf16[160,3584]{1,0:T(8,128)(2,1)} %copy-done.4, bf16[160,3584]{1,0:T(8,128)(2,1)} %copy-done.6, bf16[160,3584]{1,0:T(8,128)(2,1)} %copy-done.9, bf16[3584,1024]{1,0:T(8,128)(2,1)} %bitcast.22), custom_call_target="tpu_custom_call" | custom-call | flops 4697620480 | bytes 15000000 | tf_op jit(solution)/shard_map/pre/pallas_call | solution.py:275
  210.8 11.0 %all-to-all-done = bf16[16,80,3584]{2,1,0:T(8,128)(2,1)} async-done(((bf16[16,80,3584]{2,1,0:T(8,128)(2,1)}), bf16[16,80,3584]{2,1,0:T(8,128)(2,1)}, u32[]{:S(2)}, u32[]{:S(2)}) %all-to-all-start) | async-done | bytes 9175072 | tf_op jit(solution)/shard_map/all_to_all | solution.py:527
  221.8 34.2 %back_and_pieces.1 = bf16[1024,4608]{1,0:T(8,128)(2,1)} custom-call(s32[1]{0:T(128)} %bitcast.2.me_ref, bf16[1280,3584]{1,0:T(8,128)(2,1)} %bitcast.4.rows_ref, f32[640,1024]{1,0:T(8,128)} %pre.2.early_ref, f32[640,1024]{1,0:T(8,128)} %pre.3.late_ref, bf16[1024,3584]{1,0:T(8,128)(2,1)} %bitcast.24, bf16[3584,1024]{1,0:T(8,128)(2,1)} %bitcast.23), custom_call_target="tpu_custom_call" | custom-call | flops 18790481920 | bytes 39000000 | tf_op jit(solution)/shard_map/back_and_pieces/pallas_call | solution.py:402
  256.0 116.9 %all_to_all.15 = bf16[128,8,4608]{2,1,0:T(8,128)(2,1)} all-to-all(bf16[128,8,4608]{2,1,0:T(8,128)(2,1)} %bitcast.16), channel_id=1, replica_groups=mesh['node'=16,'local'=8] {'node','local'}, dimensions={0} | all-to-all | bytes 18874368 | tf_op jit(solution)/shard_map/all_to_all | solution.py:527
  372.9 9.4 %combine.1 = (bf16[128,3584]{1,0:T(8,128)(2,1)}, bf16[8,128]{1,0:T(8,128)(2,1)}) custom-call(s32[8,128]{1,0:T(8,128)} %bitcast.19, s32[8,128]{1,0:T(8,128)} %bitcast.20, bf16[1024,4608]{1,0:T(8,128)(2,1)} %bitcast.12, bf16[1024,4608]{1,0:T(8,128)(2,1)} %bitcast.13, bf16[1024,4608]{1,0:T(8,128)(2,1)} %bitcast.14), custom_call_target="tpu_custom_call" | custom-call | tf_op jit(solution)/shard_map/combine/pallas_call | solution.py:496
  (36 shorter events, 6.5 us)
Async XLA Ops:
  7.1 8.8 %copy-start = (bf16[128,3712]{1,0:T(8,128)(2,1)S(1)}, bf16[128,3712]{1,0:T(8,128)(2,1)}, u32[]{:S(2)}) copy-start(bf16[128,3712]{1,0:T(8,128)(2,1)} %get-tuple-element.14.refs_0_.refs_8_) | copy-start | bytes 2850820
  7.1 71.7 %all-to-all-start.1 = ((bf16[16,32,3712]{2,1,0:T(8,128)(2,1)}), bf16[16,32,3712]{2,1,0:T(8,128)(2,1)}, u32[]{:S(2)}, u32[]{:S(2)}) async-start(bf16[16,32,3712]{2,1,0:T(8,128)(2,1)} %bitcast.17), calls=%async_computation.1 | async-start | bytes 7602176 | tf_op jit(solution)/shard_map/all_to_all | solution.py:527
  15.9 22.7 %collective-permute-start.5 = (bf16[128,3712]{1,0:T(8,128)(2,1)S(1)}, bf16[128,3712]{1,0:T(8,128)(2,1)S(1)}, u32[]{:S(2)}, u32[]{:S(2)}) collective-permute-start(bf16[128,3712]{1,0:T(8,128)(2,1)S(1)} %copy-done), channel_id=1, source_target_pairs={{0,6},{1,7},{2,0},{3,1},{4,2},{5,3},{6,4},{7,5},{8,14},{9,15},{10,... | collective-permute-start | bytes 2850824 | tf_op jit(solution)/shard_map/ppermute | solution.py:534
  18.4 41.7 %collective-permute-start.3 = (bf16[128,3712]{1,0:T(8,128)(2,1)S(1)}, bf16[128,3712]{1,0:T(8,128)(2,1)S(1)}, u32[]{:S(2)}, u32[]{:S(2)}) collective-permute-start(bf16[128,3712]{1,0:T(8,128)(2,1)S(1)} %copy-done), channel_id=1, source_target_pairs={{0,4},{1,5},{2,6},{3,7},{4,0},{5,1},{6,2},{7,3},{8,12},{9,13},{10,... | collective-permute-start | bytes 2850824 | tf_op jit(solution)/shard_map/ppermute | solution.py:534
  19.0 44.4 %collective-permute-start.1 = (bf16[128,3712]{1,0:T(8,128)(2,1)S(1)}, bf16[128,3712]{1,0:T(8,128)(2,1)}, u32[]{:S(2)}, u32[]{:S(2)}) collective-permute-start(bf16[128,3712]{1,0:T(8,128)(2,1)S(1)} %copy-done), channel_id=1, source_target_pairs={{0,2},{1,3},{2,4},{3,5},{4,6},{5,7},{6,0},{7,1},{8,10},{9,11},{10,... | collective-permute-start | bytes 2850824 | tf_op jit(solution)/shard_map/ppermute | solution.py:534
  19.6 44.3 %collective-permute-start = (bf16[128,3712]{1,0:T(8,128)(2,1)S(1)}, bf16[128,3712]{1,0:T(8,128)(2,1)}, u32[]{:S(2)}, u32[]{:S(2)}) collective-permute-start(bf16[128,3712]{1,0:T(8,128)(2,1)S(1)} %copy-done), channel_id=1, source_target_pairs={{0,1},{1,0},{2,3},{3,2},{4,5},{5,4},{6,7},{7,6},{8,9},{9,8},{10,11... | collective-permute-start | bytes 2850824 | tf_op jit(solution)/shard_map/ppermute | solution.py:534
  38.6 27.8 %copy-start.1 = (bf16[128,3712]{1,0:T(8,128)(2,1)}, bf16[128,3712]{1,0:T(8,128)(2,1)S(1)}, u32[]{:S(2)}) copy-start(bf16[128,3712]{1,0:T(8,128)(2,1)S(1)} %collective-permute-done.5.refs_6_.refs_14_) | copy-start | bytes 2850820
  38.6 25.3 %collective-permute-start.6 = (bf16[128,3712]{1,0:T(8,128)(2,1)S(1)}, bf16[128,3712]{1,0:T(8,128)(2,1)}, u32[]{:S(2)}, u32[]{:S(2)}) collective-permute-start(bf16[128,3712]{1,0:T(8,128)(2,1)S(1)} %collective-permute-done.5.refs_6_.refs_14_), channel_id=1, source_target_pairs={{0,1},{1,0},{2,3},{3,2},{4,5},{5,4},{6,7},{7,6},{8,9},{9,8},{10,11... | collective-permute-start | bytes 2850824 | tf_op jit(solution)/shard_map/ppermute | solution.py:534
  60.1 6.3 %copy-start.2 = (bf16[128,3712]{1,0:T(8,128)(2,1)}, bf16[128,3712]{1,0:T(8,128)(2,1)S(1)}, u32[]{:S(2)}) copy-start(bf16[128,3712]{1,0:T(8,128)(2,1)S(1)} %collective-permute-done.3.refs_4_.refs_12_) | copy-start | bytes 2850820
  60.1 3.8 collective-permute-start.4
  63.4 3.0 collective-permute-start.2
  78.9 143.0 %all-to-all-start = ((bf16[16,80,3584]{2,1,0:T(8,128)(2,1)}), bf16[16,80,3584]{2,1,0:T(8,128)(2,1)}, u32[]{:S(2)}, u32[]{:S(2)}) async-start(bf16[16,80,3584]{2,1,0:T(8,128)(2,1)} %bitcast.15), calls=%async_computation | async-start | bytes 18350080 | tf_op jit(solution)/shard_map/all_to_all | solution.py:527
  93.8 4.9 %collective-permute-start.7 = (bf16[160,3584]{1,0:T(8,128)(2,1)}, bf16[160,3584]{1,0:T(8,128)(2,1)S(1)}, u32[]{:S(2)}, u32[]{:S(2)}) collective-permute-start(bf16[160,3584]{1,0:T(8,128)(2,1)} %get-tuple-element.17), channel_id=1, source_target_pairs={{0,1},{1,0},{2,3},{3,2},{4,5},{5,4},{6,7},{7,6},{8,9},{9,8},{10,11... | collective-permute-start | bytes 3440648 | tf_op jit(solution)/shard_map/ppermute | solution.py:534
  94.5 28.4 %collective-permute-start.8 = (bf16[160,3584]{1,0:T(8,128)(2,1)}, bf16[160,3584]{1,0:T(8,128)(2,1)S(1)}, u32[]{:S(2)}, u32[]{:S(2)}) collective-permute-start(bf16[160,3584]{1,0:T(8,128)(2,1)} %get-tuple-element.18), channel_id=1, source_target_pairs={{0,2},{1,3},{2,4},{3,5},{4,6},{5,7},{6,0},{7,1},{8,10},{9,11},{10,... | collective-permute-start | bytes 3440648 | tf_op jit(solution)/shard_map/ppermute | solution.py:534
  94.5 53.4 %collective-permute-start.9 = (bf16[160,3584]{1,0:T(8,128)(2,1)}, bf16[160,3584]{1,0:T(8,128)(2,1)S(1)}, u32[]{:S(2)}, u32[]{:S(2)}) collective-permute-start(bf16[160,3584]{1,0:T(8,128)(2,1)} %get-tuple-element.19), channel_id=1, source_target_pairs={{0,3},{1,2},{2,5},{3,4},{4,7},{5,6},{6,1},{7,0},{8,11},{9,10},{10,... | collective-permute-start | bytes 3440648 | tf_op jit(solution)/shard_map/ppermute | solution.py:534
  95.0 77.9 %collective-permute-start.10 = (bf16[160,3584]{1,0:T(8,128)(2,1)}, bf16[160,3584]{1,0:T(8,128)(2,1)S(1)}, u32[]{:S(2)}, u32[]{:S(2)}) collective-permute-start(bf16[160,3584]{1,0:T(8,128)(2,1)} %get-tuple-element.20), channel_id=1, source_target_pairs={{0,4},{1,5},{2,6},{3,7},{4,0},{5,1},{6,2},{7,3},{8,12},{9,13},{10,... | collective-permute-start | bytes 3440648 | tf_op jit(solution)/shard_map/ppermute | solution.py:534
  98.6 98.9 %collective-permute-start.11 = (bf16[160,3584]{1,0:T(8,128)(2,1)}, bf16[160,3584]{1,0:T(8,128)(2,1)S(1)}, u32[]{:S(2)}, u32[]{:S(2)}) collective-permute-start(bf16[160,3584]{1,0:T(8,128)(2,1)} %get-tuple-element.21), channel_id=1, source_target_pairs={{0,5},{1,4},{2,7},{3,6},{4,1},{5,0},{6,3},{7,2},{8,13},{9,12},{10,... | collective-permute-start | bytes 3440648 | tf_op jit(solution)/shard_map/ppermute | solution.py:534
  98.7 49.2 %copy-start.5 = (bf16[160,3584]{1,0:T(8,128)(2,1)}, bf16[160,3584]{1,0:T(8,128)(2,1)S(1)}, u32[]{:S(2)}) copy-start(bf16[160,3584]{1,0:T(8,128)(2,1)S(1)} %collective-permute-done.7.refs_1_) | copy-start | bytes 3440644
  98.7 98.8 %collective-permute-start.12 = (bf16[160,3584]{1,0:T(8,128)(2,1)}, bf16[160,3584]{1,0:T(8,128)(2,1)S(1)}, u32[]{:S(2)}, u32[]{:S(2)}) collective-permute-start(bf16[160,3584]{1,0:T(8,128)(2,1)} %get-tuple-element.22), channel_id=1, source_target_pairs={{0,6},{1,7},{2,0},{3,1},{4,2},{5,3},{6,4},{7,5},{8,14},{9,15},{10,... | collective-permute-start | bytes 3440648 | tf_op jit(solution)/shard_map/ppermute | solution.py:534
  122.9 25.1 %copy-start.7 = (bf16[160,3584]{1,0:T(8,128)(2,1)}, bf16[160,3584]{1,0:T(8,128)(2,1)S(1)}, u32[]{:S(2)}) copy-start(bf16[160,3584]{1,0:T(8,128)(2,1)S(1)} %collective-permute-done.8.refs_2_) | copy-start | bytes 3440644
  122.9 75.0 %collective-permute-start.13 = (bf16[160,3584]{1,0:T(8,128)(2,1)}, bf16[160,3584]{1,0:T(8,128)(2,1)S(1)}, u32[]{:S(2)}, u32[]{:S(2)}) collective-permute-start(bf16[160,3584]{1,0:T(8,128)(2,1)} %get-tuple-element.23), channel_id=1, source_target_pairs={{0,7},{1,6},{2,1},{3,0},{4,3},{5,2},{6,5},{7,4},{8,15},{9,14},{10,... | collective-permute-start | bytes 3440648 | tf_op jit(solution)/shard_map/ppermute | solution.py:534
  172.9 25.0 %copy-start.3 = (bf16[160,3584]{1,0:T(8,128)(2,1)}, bf16[160,3584]{1,0:T(8,128)(2,1)S(1)}, u32[]{:S(2)}) copy-start(bf16[160,3584]{1,0:T(8,128)(2,1)S(1)} %collective-permute-done.10.refs_0_) | copy-start | bytes 3440644
  197.5 1.1 copy-start.4
  197.5 1.4 copy-start.6
  (2 other events, 2.1 us)

commit v4 on v3

--- a/solution.py
+++ b/solution.py
@@ -80,7 +80,7 @@
     top, tok = ids_t.shape
     width = x.shape[1]
     share = tok * NODES_MAX // nodes
-    steps = 4
+    steps = 2
     part = tok // steps
     return pl.pallas_call(
         functools.partial(node_kernel, share=share, nodes=nodes, local=local),
@@ -149,11 +149,12 @@
     total, wide = rows.shape
     width = wide - EXTRA
     share = total // nodes
-    fold = width // QUARTERS
+    steps = 2
+    fold = width // steps
     size = nodes * CAP
     return pl.pallas_call(
         functools.partial(part_kernel, share=share, nodes=nodes, local=local),
-        grid=(QUARTERS,),
+        grid=(steps,),
         in_specs=[
             pl.BlockSpec(memory_space=pltpu.SMEM),
             pl.BlockSpec((total, fold), lambda i: (0, i)),
@@ -222,7 +223,7 @@
 def gathered_rows(me, parts, nodes, local):
     tok, wide = parts[0].shape
     width = wide - EXTRA
-    tile = width // 7
+    tile = width // 2
     size = nodes * local * CAP
     picks = pltpu.VMEM((local // 2, nodes * 2 * MAIN, 2 * tok), BF16)
     return pl.pallas_call(

time: 383 us -> 379 us (0.990)
  Pallas kernels: 92.4 us -> 87.6 us
  transfers between devices with their start and end apart: 16 -> 16, of which waited for: 9 -> 9; matrix products, arithmetic and copies ran while one was open for 0% -> 0% of each run, Pallas kernels for 11% -> 10%
where the time goes in v4:
time: 379 us; the launch traced here: 378 us
  waiting for transfers between devices  118 us (31%)
  blocking collectives  117 us (31%)
  Pallas kernels  87.6 us (23%)
  starting transfers between devices  52 us (14%)
    all_to_all x1, blocking collectives, exchange(): lax.all_to_all(blocks, axes, split_axis=0, concat_axis=0, tiled=True)  117 us
    ppermute x14, waiting for transfers between devices, shift(): return lax.ppermute(rows, 'local', pairs)  106 us
    ppermute x14, starting transfers between devices, shift(): return lax.ppermute(rows, 'local', pairs)  36.6 us
    pallas_call x1, Pallas kernels, pieces_of(): pl.pallas_call(functools.partial(back_kernel, local=local), grid=(first +...  34.2 us
    pallas_call x2, Pallas kernels, pre_of(): pl.pallas_call(functools.partial(pre_kernel, nodes=nodes), grid=(hid // t...  21.6 us
    all_to_all x2, starting transfers between devices, exchange(): lax.all_to_all(blocks, axes, split_axis=0, concat_axis=0, tiled=True)  15.4 us
    all_to_all x2, waiting for transfers between devices, exchange(): lax.all_to_all(blocks, axes, split_axis=0, concat_axis=0, tiled=True)  11.9 us
    pallas_call x1, Pallas kernels, gathered_rows(): pl.pallas_call(functools.partial(gathered_kernel, tok=tok, nodes=nodes, l...  9.79 us
  transfers between devices with their start and end apart: 16, of which 9 were waited for; matrix products, arithmetic and copies ran while one was open for 0% of the time, Pallas kernels for 10%

profile of v4, /device:TPU:1, one launch (start us, length us, event | category | flops | bytes accessed | tf_op | source)
XLA Modules:
  0.0 378.3 jit_solution(9786071702390877485)
XLA Ops:
  0.6 5.2 %node_rows.1 = (bf16[512,3712]{1,0:T(8,128)(2,1)}, bf16[128,3712]{1,0:T(8,128)(2,1)}) custom-call(s32[8,128]{1,0:T(8,128)} %bitcast.18, bf16[128,3584]{1,0:T(8,128)(2,1)} %x_ref.1, bf16[128,3584]{1,0:T(8,128)(2,1)} %dy_ref.1), custom_call_target="tpu_custom_call" | custom-call | flops 939524096 | bytes 7000000 | tf_op jit(solution)/shard_map/node_rows/pallas_call | solution.py:85
  5.8 8.8 %all-to-all-start.1 = ((bf16[16,32,3712]{2,1,0:T(8,128)(2,1)}), bf16[16,32,3712]{2,1,0:T(8,128)(2,1)}, u32[]{:S(2)}, u32[]{:S(2)}) async-start(bf16[16,32,3712]{2,1,0:T(8,128)(2,1)} %bitcast.17), calls=%async_computation.1 | async-start | bytes 7602176 | tf_op jit(solution)/shard_map/all_to_all | solution.py:528
  14.6 2.5 collective-permute-start.5
  18.3 1.8 collective-permute-start
  20.1 17.3 %collective-permute-done.5.refs_6_.refs_14_ = bf16[128,3712]{1,0:T(8,128)(2,1)S(1)} collective-permute-done((bf16[128,3712]{1,0:T(8,128)(2,1)S(1)}, bf16[128,3712]{1,0:T(8,128)(2,1)S(1)}, u32[]{:S(2)}, u32[]{:S(2)}) %collective-permute-start.5) | collective-permute-done | bytes 950304 | tf_op jit(solution)/shard_map/ppermute | solution.py:535
  37.4 21.5 %collective-permute-start.6 = (bf16[128,3712]{1,0:T(8,128)(2,1)S(1)}, bf16[128,3712]{1,0:T(8,128)(2,1)}, u32[]{:S(2)}, u32[]{:S(2)}) collective-permute-start(bf16[128,3712]{1,0:T(8,128)(2,1)S(1)} %collective-permute-done.5.refs_6_.refs_14_), channel_id=1, source_target_pairs={{0,1},{1,0},{2,3},{3,2},{4,5},{5,4},{6,7},{7,6},{8,9},{9,8},{10,11... | collective-permute-start | bytes 2850824 | tf_op jit(solution)/shard_map/ppermute | solution.py:535
  58.9 3.2 collective-permute-done.1.refs_2_.refs_10_
  62.6 2.5 collective-permute-done.2.refs_3_.refs_11_
  65.1 9.8 %gathered_rows.1 = bf16[1280,3584]{1,0:T(8,128)(2,1)} custom-call(s32[1]{0:T(128)} %bitcast.2.me_ref, bf16[128,3712]{1,0:T(8,128)(2,1)} %get-tuple-element.14.refs_0_.refs_8_, bf16[128,3712]{1,0:T(8,128)(2,1)} %collective-permute-done.refs_1_.refs_9_, bf16[128,3712]{1,0:T(8,128)(2,1)} %collective-permute-done.1.refs_2_.refs_10_, ...), custom_call_target="tpu_custom_call" | custom-call | flops 4697620480 | bytes 17000000 | tf_op jit(solution)/shard_map/gathered_rows/pallas_call | solution.py:229
  74.9 6.7 %all-to-all-start = ((bf16[16,80,3584]{2,1,0:T(8,128)(2,1)}), bf16[16,80,3584]{2,1,0:T(8,128)(2,1)}, u32[]{:S(2)}, u32[]{:S(2)}) async-start(bf16[16,80,3584]{2,1,0:T(8,128)(2,1)} %bitcast.15), calls=%async_computation | async-start | bytes 18350080 | tf_op jit(solution)/shard_map/all_to_all | solution.py:528
  81.6 7.5 %part_rows.1 = (bf16[160,3584]{1,0:T(8,128)(2,1)}, bf16[160,3584]{1,0:T(8,128)(2,1)}, bf16[160,3584]{1,0:T(8,128)(2,1)}, bf16[160,3584]{1,0:T(8,128)(2,1)}, bf16...) custom-call(s32[1]{0:T(128)} %bitcast.2.me_ref, ...), custom_call_target="tpu_custom_call" | custom-call | flops 4697620480 | bytes 13000000 | tf_op jit(solution)/shard_map/part_rows/pallas_call | solution.py:155
  90.2 3.7 collective-permute-start.10
  93.9 2.1 collective-permute-start.12
  96.0 22.1 %collective-permute-done.8.refs_2_ = bf16[160,3584]{1,0:T(8,128)(2,1)S(1)} collective-permute-done((bf16[160,3584]{1,0:T(8,128)(2,1)}, bf16[160,3584]{1,0:T(8,128)(2,1)S(1)}, u32[]{:S(2)}, u32[]{:S(2)}) %collective-permute-start.8) | collective-permute-done | bytes 1146912 | tf_op jit(solution)/shard_map/ppermute | solution.py:535
  118.1 2.2 collective-permute-start.13
  120.3 22.8 %collective-permute-done.9.refs_3_ = bf16[160,3584]{1,0:T(8,128)(2,1)S(1)} collective-permute-done((bf16[160,3584]{1,0:T(8,128)(2,1)}, bf16[160,3584]{1,0:T(8,128)(2,1)S(1)}, u32[]{:S(2)}, u32[]{:S(2)}) %collective-permute-start.9) | collective-permute-done | bytes 1146912 | tf_op jit(solution)/shard_map/ppermute | solution.py:535
  144.2 10.8 %pre.2.early_ref = f32[640,1024]{1,0:T(8,128)} custom-call(bf16[160,3584]{1,0:T(8,128)(2,1)} %get-tuple-element.16.refs_0_, bf16[160,3584]{1,0:T(8,128)(2,1)} %copy-done.5, bf16[160,3584]{1,0:T(8,128)(2,1)} %copy-done.7, bf16[160,3584]{1,0:T(8,128)(2,1)} %copy-done.8, bf16[3584,1024]{1,0:T(8,128)(2,1)} %bitcast.21), custom_call_target="tpu_custom_call" | custom-call | flops 4697620480 | bytes 15000000 | tf_op jit(solution)/shard_map/pre/pallas_call | solution.py:276
  155.0 13.1 %collective-permute-done.10.refs_0_ = bf16[160,3584]{1,0:T(8,128)(2,1)S(1)} collective-permute-done((bf16[160,3584]{1,0:T(8,128)(2,1)}, bf16[160,3584]{1,0:T(8,128)(2,1)S(1)}, u32[]{:S(2)}, u32[]{:S(2)}) %collective-permute-start.10) | collective-permute-done | bytes 1146912 | tf_op jit(solution)/shard_map/ppermute | solution.py:535
  168.1 24.6 %collective-permute-done.11.refs_1_ = bf16[160,3584]{1,0:T(8,128)(2,1)S(1)} collective-permute-done((bf16[160,3584]{1,0:T(8,128)(2,1)}, bf16[160,3584]{1,0:T(8,128)(2,1)S(1)}, u32[]{:S(2)}, u32[]{:S(2)}) %collective-permute-start.11) | collective-permute-done | bytes 1146912 | tf_op jit(solution)/shard_map/ppermute | solution.py:535
  195.2 10.8 %pre.3.late_ref = f32[640,1024]{1,0:T(8,128)} custom-call(bf16[160,3584]{1,0:T(8,128)(2,1)} %copy-done.3, bf16[160,3584]{1,0:T(8,128)(2,1)} %copy-done.4, bf16[160,3584]{1,0:T(8,128)(2,1)} %copy-done.6, bf16[160,3584]{1,0:T(8,128)(2,1)} %copy-done.9, bf16[3584,1024]{1,0:T(8,128)(2,1)} %bitcast.22), custom_call_target="tpu_custom_call" | custom-call | flops 4697620480 | bytes 15000000 | tf_op jit(solution)/shard_map/pre/pallas_call | solution.py:276
  206.0 11.9 %all-to-all-done = bf16[16,80,3584]{2,1,0:T(8,128)(2,1)} async-done(((bf16[16,80,3584]{2,1,0:T(8,128)(2,1)}), bf16[16,80,3584]{2,1,0:T(8,128)(2,1)}, u32[]{:S(2)}, u32[]{:S(2)}) %all-to-all-start) | async-done | bytes 9175072 | tf_op jit(solution)/shard_map/all_to_all | solution.py:528
  217.9 34.2 %back_and_pieces.1 = bf16[1024,4608]{1,0:T(8,128)(2,1)} custom-call(s32[1]{0:T(128)} %bitcast.2.me_ref, bf16[1280,3584]{1,0:T(8,128)(2,1)} %bitcast.4.rows_ref, f32[640,1024]{1,0:T(8,128)} %pre.2.early_ref, f32[640,1024]{1,0:T(8,128)} %pre.3.late_ref, bf16[1024,3584]{1,0:T(8,128)(2,1)} %bitcast.24, bf16[3584,1024]{1,0:T(8,128)(2,1)} %bitcast.23), custom_call_target="tpu_custom_call" | custom-call | flops 18790481920 | bytes 39000000 | tf_op jit(solution)/shard_map/back_and_pieces/pallas_call | solution.py:403
  252.1 116.8 %all_to_all.15 = bf16[128,8,4608]{2,1,0:T(8,128)(2,1)} all-to-all(bf16[128,8,4608]{2,1,0:T(8,128)(2,1)} %bitcast.16), channel_id=1, replica_groups=mesh['node'=16,'local'=8] {'node','local'}, dimensions={0} | all-to-all | bytes 18874368 | tf_op jit(solution)/shard_map/all_to_all | solution.py:528
  368.9 9.4 %combine.1 = (bf16[128,3584]{1,0:T(8,128)(2,1)}, bf16[8,128]{1,0:T(8,128)(2,1)}) custom-call(s32[8,128]{1,0:T(8,128)} %bitcast.19, s32[8,128]{1,0:T(8,128)} %bitcast.20, bf16[1024,4608]{1,0:T(8,128)(2,1)} %bitcast.12, bf16[1024,4608]{1,0:T(8,128)(2,1)} %bitcast.13, bf16[1024,4608]{1,0:T(8,128)(2,1)} %bitcast.14), custom_call_target="tpu_custom_call" | custom-call | tf_op jit(solution)/shard_map/combine/pallas_call | solution.py:497
  (36 shorter events, 6.4 us)
Async XLA Ops:
  5.8 8.8 %copy-start = (bf16[128,3712]{1,0:T(8,128)(2,1)S(1)}, bf16[128,3712]{1,0:T(8,128)(2,1)}, u32[]{:S(2)}) copy-start(bf16[128,3712]{1,0:T(8,128)(2,1)} %get-tuple-element.14.refs_0_.refs_8_) | copy-start | bytes 2850820
  5.8 69.1 %all-to-all-start.1 = ((bf16[16,32,3712]{2,1,0:T(8,128)(2,1)}), bf16[16,32,3712]{2,1,0:T(8,128)(2,1)}, u32[]{:S(2)}, u32[]{:S(2)}) async-start(bf16[16,32,3712]{2,1,0:T(8,128)(2,1)} %bitcast.17), calls=%async_computation.1 | async-start | bytes 7602176 | tf_op jit(solution)/shard_map/all_to_all | solution.py:528
  14.6 22.8 %collective-permute-start.5 = (bf16[128,3712]{1,0:T(8,128)(2,1)S(1)}, bf16[128,3712]{1,0:T(8,128)(2,1)S(1)}, u32[]{:S(2)}, u32[]{:S(2)}) collective-permute-start(bf16[128,3712]{1,0:T(8,128)(2,1)S(1)} %copy-done), channel_id=1, source_target_pairs={{0,6},{1,7},{2,0},{3,1},{4,2},{5,3},{6,4},{7,5},{8,14},{9,15},{10,... | collective-permute-start | bytes 2850824 | tf_op jit(solution)/shard_map/ppermute | solution.py:535
  17.2 41.7 %collective-permute-start.3 = (bf16[128,3712]{1,0:T(8,128)(2,1)S(1)}, bf16[128,3712]{1,0:T(8,128)(2,1)S(1)}, u32[]{:S(2)}, u32[]{:S(2)}) collective-permute-start(bf16[128,3712]{1,0:T(8,128)(2,1)S(1)} %copy-done), channel_id=1, source_target_pairs={{0,4},{1,5},{2,6},{3,7},{4,0},{5,1},{6,2},{7,3},{8,12},{9,13},{10,... | collective-permute-start | bytes 2850824 | tf_op jit(solution)/shard_map/ppermute | solution.py:535
  17.7 44.4 %collective-permute-start.1 = (bf16[128,3712]{1,0:T(8,128)(2,1)S(1)}, bf16[128,3712]{1,0:T(8,128)(2,1)}, u32[]{:S(2)}, u32[]{:S(2)}) collective-permute-start(bf16[128,3712]{1,0:T(8,128)(2,1)S(1)} %copy-done), channel_id=1, source_target_pairs={{0,2},{1,3},{2,4},{3,5},{4,6},{5,7},{6,0},{7,1},{8,10},{9,11},{10,... | collective-permute-start | bytes 2850824 | tf_op jit(solution)/shard_map/ppermute | solution.py:535
  18.3 44.3 %collective-permute-start = (bf16[128,3712]{1,0:T(8,128)(2,1)S(1)}, bf16[128,3712]{1,0:T(8,128)(2,1)}, u32[]{:S(2)}, u32[]{:S(2)}) collective-permute-start(bf16[128,3712]{1,0:T(8,128)(2,1)S(1)} %copy-done), channel_id=1, source_target_pairs={{0,1},{1,0},{2,3},{3,2},{4,5},{5,4},{6,7},{7,6},{8,9},{9,8},{10,11... | collective-permute-start | bytes 2850824 | tf_op jit(solution)/shard_map/ppermute | solution.py:535
  37.4 27.7 %copy-start.1 = (bf16[128,3712]{1,0:T(8,128)(2,1)}, bf16[128,3712]{1,0:T(8,128)(2,1)S(1)}, u32[]{:S(2)}) copy-start(bf16[128,3712]{1,0:T(8,128)(2,1)S(1)} %collective-permute-done.5.refs_6_.refs_14_) | copy-start | bytes 2850820
  37.4 25.2 %collective-permute-start.6 = (bf16[128,3712]{1,0:T(8,128)(2,1)S(1)}, bf16[128,3712]{1,0:T(8,128)(2,1)}, u32[]{:S(2)}, u32[]{:S(2)}) collective-permute-start(bf16[128,3712]{1,0:T(8,128)(2,1)S(1)} %collective-permute-done.5.refs_6_.refs_14_), channel_id=1, source_target_pairs={{0,1},{1,0},{2,3},{3,2},{4,5},{5,4},{6,7},{7,6},{8,9},{9,8},{10,11... | collective-permute-start | bytes 2850824 | tf_op jit(solution)/shard_map/ppermute | solution.py:535
  58.8 6.3 %copy-start.2 = (bf16[128,3712]{1,0:T(8,128)(2,1)}, bf16[128,3712]{1,0:T(8,128)(2,1)S(1)}, u32[]{:S(2)}) copy-start(bf16[128,3712]{1,0:T(8,128)(2,1)S(1)} %collective-permute-done.3.refs_4_.refs_12_) | copy-start | bytes 2850820
  58.8 3.8 collective-permute-start.4
  62.1 3.0 collective-permute-start.2
  74.9 143.0 %all-to-all-start = ((bf16[16,80,3584]{2,1,0:T(8,128)(2,1)}), bf16[16,80,3584]{2,1,0:T(8,128)(2,1)}, u32[]{:S(2)}, u32[]{:S(2)}) async-start(bf16[16,80,3584]{2,1,0:T(8,128)(2,1)} %bitcast.15), calls=%async_computation | async-start | bytes 18350080 | tf_op jit(solution)/shard_map/all_to_all | solution.py:528
  89.1 4.8 %collective-permute-start.7 = (bf16[160,3584]{1,0:T(8,128)(2,1)}, bf16[160,3584]{1,0:T(8,128)(2,1)S(1)}, u32[]{:S(2)}, u32[]{:S(2)}) collective-permute-start(bf16[160,3584]{1,0:T(8,128)(2,1)} %get-tuple-element.17), channel_id=1, source_target_pairs={{0,1},{1,0},{2,3},{3,2},{4,5},{5,4},{6,7},{7,6},{8,9},{9,8},{10,11... | collective-permute-start | bytes 3440648 | tf_op jit(solution)/shard_map/ppermute | solution.py:535
  89.7 28.4 %collective-permute-start.8 = (bf16[160,3584]{1,0:T(8,128)(2,1)}, bf16[160,3584]{1,0:T(8,128)(2,1)S(1)}, u32[]{:S(2)}, u32[]{:S(2)}) collective-permute-start(bf16[160,3584]{1,0:T(8,128)(2,1)} %get-tuple-element.18), channel_id=1, source_target_pairs={{0,2},{1,3},{2,4},{3,5},{4,6},{5,7},{6,0},{7,1},{8,10},{9,11},{10,... | collective-permute-start | bytes 3440648 | tf_op jit(solution)/shard_map/ppermute | solution.py:535
  89.7 53.4 %collective-permute-start.9 = (bf16[160,3584]{1,0:T(8,128)(2,1)}, bf16[160,3584]{1,0:T(8,128)(2,1)S(1)}, u32[]{:S(2)}, u32[]{:S(2)}) collective-permute-start(bf16[160,3584]{1,0:T(8,128)(2,1)} %get-tuple-element.19), channel_id=1, source_target_pairs={{0,3},{1,2},{2,5},{3,4},{4,7},{5,6},{6,1},{7,0},{8,11},{9,10},{10,... | collective-permute-start | bytes 3440648 | tf_op jit(solution)/shard_map/ppermute | solution.py:535
  90.2 77.9 %collective-permute-start.10 = (bf16[160,3584]{1,0:T(8,128)(2,1)}, bf16[160,3584]{1,0:T(8,128)(2,1)S(1)}, u32[]{:S(2)}, u32[]{:S(2)}) collective-permute-start(bf16[160,3584]{1,0:T(8,128)(2,1)} %get-tuple-element.20), channel_id=1, source_target_pairs={{0,4},{1,5},{2,6},{3,7},{4,0},{5,1},{6,2},{7,3},{8,12},{9,13},{10,... | collective-permute-start | bytes 3440648 | tf_op jit(solution)/shard_map/ppermute | solution.py:535
  93.8 98.9 %collective-permute-start.11 = (bf16[160,3584]{1,0:T(8,128)(2,1)}, bf16[160,3584]{1,0:T(8,128)(2,1)S(1)}, u32[]{:S(2)}, u32[]{:S(2)}) collective-permute-start(bf16[160,3584]{1,0:T(8,128)(2,1)} %get-tuple-element.21), channel_id=1, source_target_pairs={{0,5},{1,4},{2,7},{3,6},{4,1},{5,0},{6,3},{7,2},{8,13},{9,12},{10,... | collective-permute-start | bytes 3440648 | tf_op jit(solution)/shard_map/ppermute | solution.py:535
  93.9 49.2 %copy-start.5 = (bf16[160,3584]{1,0:T(8,128)(2,1)}, bf16[160,3584]{1,0:T(8,128)(2,1)S(1)}, u32[]{:S(2)}) copy-start(bf16[160,3584]{1,0:T(8,128)(2,1)S(1)} %collective-permute-done.7.refs_1_) | copy-start | bytes 3440644
  93.9 98.8 %collective-permute-start.12 = (bf16[160,3584]{1,0:T(8,128)(2,1)}, bf16[160,3584]{1,0:T(8,128)(2,1)S(1)}, u32[]{:S(2)}, u32[]{:S(2)}) collective-permute-start(bf16[160,3584]{1,0:T(8,128)(2,1)} %get-tuple-element.22), channel_id=1, source_target_pairs={{0,6},{1,7},{2,0},{3,1},{4,2},{5,3},{6,4},{7,5},{8,14},{9,15},{10,... | collective-permute-start | bytes 3440648 | tf_op jit(solution)/shard_map/ppermute | solution.py:535
  118.1 25.0 %copy-start.7 = (bf16[160,3584]{1,0:T(8,128)(2,1)}, bf16[160,3584]{1,0:T(8,128)(2,1)S(1)}, u32[]{:S(2)}) copy-start(bf16[160,3584]{1,0:T(8,128)(2,1)S(1)} %collective-permute-done.8.refs_2_) | copy-start | bytes 3440644
  118.1 75.0 %collective-permute-start.13 = (bf16[160,3584]{1,0:T(8,128)(2,1)}, bf16[160,3584]{1,0:T(8,128)(2,1)S(1)}, u32[]{:S(2)}, u32[]{:S(2)}) collective-permute-start(bf16[160,3584]{1,0:T(8,128)(2,1)} %get-tuple-element.23), channel_id=1, source_target_pairs={{0,7},{1,6},{2,1},{3,0},{4,3},{5,2},{6,5},{7,4},{8,15},{9,14},{10,... | collective-permute-start | bytes 3440648 | tf_op jit(solution)/shard_map/ppermute | solution.py:535
  168.1 25.0 %copy-start.3 = (bf16[160,3584]{1,0:T(8,128)(2,1)}, bf16[160,3584]{1,0:T(8,128)(2,1)S(1)}, u32[]{:S(2)}) copy-start(bf16[160,3584]{1,0:T(8,128)(2,1)S(1)} %collective-permute-done.10.refs_0_) | copy-start | bytes 3440644
  192.7 1.1 copy-start.4
  192.7 1.4 copy-start.6
  (2 other events, 2.1 us)
